TPU v7x, 32 devices: a whole 2x2x4 slice. The times are simulated.
32 devices in a mesh: section: 2 (over core), row: 4 (over z), col: 4 (over y, x).
Axes of the slice: x: 2, y: 2, z: 4, core: 2. Of those that a mesh axis runs over, the one named last changes fastest.
Arguments:
- tokens_in: bfloat16 [2, 1024, 2048], P(None, 'row', 'col'), may hold values from -6 to 6
- out_grad: bfloat16 [2, 1024, 2048], P(None, 'row', 'col'), may hold values from -6 to 6
- segments: int32 [2, 1024], P(None, 'row'), may hold values from 0 to 3, as said below
- positions: int32 [2, 1024], P(None, 'row'), may hold values from 0 to 511, as said below
- w_qkv: bfloat16 [2, 2048, 3, 2048], P('section', 'row', None, 'col'), may hold values from -0.125 to 0.125
- b_qkv: bfloat16 [2, 3, 2048], P('section', None, 'col'), may hold values from -4 to 4
- w_out: bfloat16 [2, 2048, 2048], P('section', 'row', 'col'), may hold values from -0.75 to 0.75
- w_gate_up: bfloat16 [2, 2048, 2, 5632], P('section', 'row', None, 'col'), may hold values from -0.125 to 0.125
- w_down: bfloat16 [2, 5632, 2048], P('section', 'row', 'col'), may hold values from -0.109375 to 0.109375
- norm_gains: bfloat16 [2, 2, 2048], P('section', None, 'col'), may hold values from 0.5 to 1.5
- norm_biases: bfloat16 [2, 2, 2048], P('section', None, 'col'), may hold values from -4 to 4
Outputs:
- layer_outputs: float32 [2, 2, 1024, 2048], P('section', None, 'row', 'col')
- input_grads: float32 [2, 2, 1024, 2048], P('section', None, 'row', 'col')
- grad_qkv: float32 [2, 2048, 3, 2048], P('section', 'row', None, 'col')
- grad_qkv_bias: float32 [2, 3, 2048], P('section', None, 'col')
- grad_out: float32 [2, 2048, 2048], P('section', 'row', 'col')
- grad_gate_up: float32 [2, 2048, 2, 5632], P('section', 'row', None, 'col')
- grad_down: float32 [2, 5632, 2048], P('section', 'row', 'col')
- grad_norm_gains: float32 [2, 2, 2048], P('section', None, 'col')
- grad_norm_biases: float32 [2, 2, 2048], P('section', None, 'col')
Inputs may be any that keep to these rules, and one draw needn't show every extreme that they name: `segments`: in each sequence (each aligned block of 256 tokens of a micro-batch) segment numbers start at 0, never fall and take every value up to 3. Within a document positions rise by one from token to token; the first document of each sequence starts at position 0, documents between the first and the last at a position below 256, and the last document of each sequence ends at position 511.
All inputs are finite; a program needn't handle non-finite values.
Results may differ from a plain program's by a relative error of at most 0.018.
Values may be sent and summed in bfloat16 or wider, within the bound.
No kernel may reach another device: no remote copies, remote signals or barrier semaphores. Data moves between devices by JAX's collectives and lax.ppermute only.
A program may use at most 256 MiB of HBM per device.

v0:
```python
import jax
import jax.numpy as jnp
from jax import lax
from jax.experimental import pallas as pl
from jax.experimental.pallas import tpu as pltpu
from jax.sharding import PartitionSpec as P

HEAD_DIM = 64
ROT = 16
NORM_EPSILON = 1e-05
ROPE_BASE = 10000.0
SCORE_SCALE = 0.125
MASKED_SCORE = -1e30
BF = jnp.bfloat16
F32 = jnp.float32


def trade(stack, axis):
    return lax.all_to_all(stack, axis, split_axis=0, concat_axis=0)


def gather(value, axis):
    return trade(jnp.broadcast_to(value, (lax.axis_size(axis), *value.shape)), axis)


def total(stack, axis):
    return jnp.sum(trade(stack, axis).astype(F32), axis=0)


def tie(point, *values):
    return lax.optimization_barrier((point, *values))


def dot(a, b):
    return lax.dot_general(a, b, (((1,), (0,)), ((), ())), preferred_element_type=F32)


def dot_nt(a, b):
    return lax.dot_general(a, b, (((1,), (1,)), ((), ())), preferred_element_type=F32)


def dot_tn(a, b):
    return lax.dot_general(a, b, (((0,), (0,)), ((), ())), preferred_element_type=F32)


def norm(values, gain, shift):
    mean_value = jnp.mean(values, axis=-1, keepdims=True)
    centred = values - mean_value
    variance = jnp.mean(centred * centred, axis=-1, keepdims=True)
    inv = lax.rsqrt(variance + NORM_EPSILON)
    scaled = centred * inv
    return (scaled * gain + shift).astype(BF), scaled, inv


def norm_back(grad, scaled, inv, gain):
    e = grad * gain
    mean_e = jnp.mean(e, axis=-1, keepdims=True)
    mean_p = jnp.mean(e * scaled, axis=-1, keepdims=True)
    return inv * (e - mean_e - scaled * mean_p), jnp.sum(grad * scaled, axis=0), jnp.sum(grad, axis=0)


def call(body, grid, in_specs, out_specs, out_shape, scratch, flops, moved, table, *args):
    return pl.pallas_call(
        body,
        grid_spec=pltpu.PrefetchScalarGridSpec(
            num_scalar_prefetch=1,
            grid=(grid,),
            in_specs=in_specs,
            out_specs=out_specs,
            scratch_shapes=scratch,
        ),
        out_shape=out_shape,
        compiler_params=pltpu.CompilerParams(vmem_limit_bytes=56 * 2**20),
        cost_estimate=pl.CostEstimate(flops=int(flops), bytes_accessed=int(moved), transcendentals=0),
    )(table, *args)


def no_table():
    return jnp.zeros((1, 1), jnp.int32)


def turn(x, cosines, sines, sign):
    ahead = pltpu.roll(x, 128 - ROT // 2, 1)
    behind = pltpu.roll(x, ROT // 2, 1)
    return x * cosines + sign * (ahead * sines[0] + behind * sines[1])


def head_lanes(n):
    lanes = lax.broadcasted_iota(jnp.int32, (n, 128), 1)
    return lanes < HEAD_DIM


def softmax_of(q, k, allowed):
    scores = jnp.where(allowed, dot_nt(q, k) * SCORE_SCALE, MASKED_SCORE)
    shifted = jnp.exp(scores - jnp.max(scores, axis=1, keepdims=True))
    return shifted / jnp.sum(shifted, axis=1, keepdims=True)


def whole(*shape):
    return pl.BlockSpec(shape, lambda i, t: (0,) * len(shape))


HBM = pl.BlockSpec(memory_space=pl.ANY)


def fetch(pairs, sems):
    copies = [pltpu.make_async_copy(src, dst, sems.at[i]) for i, (src, dst) in enumerate(pairs)]
    for copy in copies:
        copy.start()
    return copies


def attention(a, w, bias, tables, mask):
    n, width = a.shape
    m = w.shape[1] // 4
    half = width // 2

    def body(_, a_ref, w_ref, bias_ref, tab_ref, mask_ref, qkv_ref, o_ref, held, acc, sems):
        parts = [pl.ds(i * half, half) for i in range(2)]
        copies = fetch([(w_ref.at[part, pl.ds(0, 3 * m)], held.at[part]) for part in parts], sems)
        copies[0].wait()
        acc[...] = dot(a_ref[:, :half], held[:half]) + bias_ref[...]
        copies[1].wait()
        acc[...] += dot(a_ref[:, half:], held[half:])
        low = head_lanes(n)
        zero = jnp.zeros((n, 128), BF)
        allowed = mask_ref[...] > 0
        cosines, sines = tab_ref[0], (tab_ref[1], tab_ref[2])
        for pair in range(m // 128):
            at = pair * 128
            q = turn(acc[:, at : at + 128], cosines, sines, 1.0).astype(BF)
            k = turn(acc[:, m + at : m + at + 128], cosines, sines, 1.0).astype(BF)
            v = acc[:, 2 * m + at : 2 * m + at + 128].astype(BF)
            qkv_ref[:, at : at + 128] = q
            qkv_ref[:, m + at : m + at + 128] = k
            qkv_ref[:, 2 * m + at : 2 * m + at + 128] = v
            p0 = softmax_of(jnp.where(low, q, zero), k, allowed).astype(BF)
            p1 = softmax_of(jnp.where(low, zero, q), k, allowed).astype(BF)
            o_ref[:, at : at + 128] = jnp.where(low, dot(p0, v), dot(p1, v)).astype(BF)

    return call(
        body,
        1,
        [whole(n, width), HBM, whole(1, 3 * m), whole(3, n, 128), whole(n, n)],
        [whole(n, 3 * m), whole(n, m)],
        [jax.ShapeDtypeStruct((n, 3 * m), BF), jax.ShapeDtypeStruct((n, m), BF)],
        [pltpu.VMEM((width, 3 * m), BF), pltpu.VMEM((n, 3 * m), F32), pltpu.SemaphoreType.DMA((2,))],
        2 * n * width * 3 * m,
        2 * width * 3 * m,
        no_table(),
        a,
        w,
        bias,
        tables,
        mask,
    )


def attention_back(d_o, qkv, w, tables, mask):
    n, m = d_o.shape
    width = w.shape[0]
    half = width // 2

    def body(_, d_ref, qkv_ref, w_ref, tab_ref, mask_ref, dp_ref, sum_ref, da_ref, held, sems):
        parts = [pl.ds(i * half, half) for i in range(2)]
        copies = fetch([(w_ref.at[part, pl.ds(0, 3 * m)], held.at[part]) for part in parts], sems)
        low = head_lanes(n)
        zero = jnp.zeros((n, 128), BF)
        allowed = mask_ref[...] > 0
        cosines, sines = tab_ref[0], (tab_ref[1], tab_ref[2])
        for pair in range(m // 128):
            at = pair * 128
            q = qkv_ref[:, at : at + 128]
            k = qkv_ref[:, m + at : m + at + 128]
            v = qkv_ref[:, 2 * m + at : 2 * m + at + 128]
            g = d_ref[:, at : at + 128]
            out = []
            for mine in (True, False):
                pick_q = jnp.where(low, q, zero) if mine else jnp.where(low, zero, q)
                pick_g = jnp.where(low, g, zero) if mine else jnp.where(low, zero, g)
                probs = softmax_of(pick_q, k, allowed)
                d_probs = dot_nt(pick_g, v)
                row = jnp.sum(d_probs * probs, axis=1, keepdims=True)
                ds = (probs * (d_probs - row)).astype(BF)
                out.append((dot(ds, k), dot_tn(ds, q), dot_tn(probs.astype(BF), g)))
            dq, dk, dv = (jnp.where(low, x, y) for x, y in zip(*out))
            dq = turn(dq * SCORE_SCALE, cosines, sines, -1.0)
            dk = turn(dk * SCORE_SCALE, cosines, sines, -1.0)
            for place, part in enumerate((dq, dk, dv)):
                part = part.astype(BF)
                dp_ref[:, place * m + at : place * m + at + 128] = part
                sum_ref[:, place * m + at : place * m + at + 128] = jnp.sum(part.astype(F32), axis=0, keepdims=True)
        for i, copy in enumerate(copies):
            copy.wait()
            da_ref[:, i * half : (i + 1) * half] = dot_nt(dp_ref[...], held[i * half : (i + 1) * half]).astype(BF)

    return call(
        body,
        1,
        [whole(n, m), whole(n, 3 * m), HBM, whole(3, n, 128), whole(n, n)],
        [whole(n, 3 * m), whole(1, 3 * m), whole(n, width)],
        [
            jax.ShapeDtypeStruct((n, 3 * m), BF),
            jax.ShapeDtypeStruct((1, 3 * m), F32),
            jax.ShapeDtypeStruct((n, width), BF),
        ],
        [pltpu.VMEM((width, 3 * m), BF), pltpu.SemaphoreType.DMA((2,))],
        2 * n * width * 3 * m,
        2 * width * 3 * m,
        no_table(),
        d_o,
        qkv,
        w,
        tables,
        mask,
    )


def heads_out(o, w):
    c, n, m = o.shape

    def body(_, o_ref, w_ref, out_ref, held, sems):
        (copy,) = fetch([(w_ref.at[:, pl.ds(3 * m, m)], held)], sems)
        o_wide = jnp.concatenate([o_ref[i] for i in range(c)], axis=1)
        copy.wait()
        out_ref[...] = dot(o_wide, held[...]).astype(BF)

    return call(
        body,
        1,
        [whole(c, n, m), HBM],
        whole(n, m),
        jax.ShapeDtypeStruct((n, m), BF),
        [pltpu.VMEM((c * m, m), BF), pltpu.SemaphoreType.DMA((1,))],
        2 * c * n * m * m,
        2 * c * m * m,
        no_table(),
        o,
        w,
    )


def heads_back(d_h, w):
    n, m = d_h.shape
    c = w.shape[0] // m

    def body(_, d_ref, w_ref, out_ref, held, sems):
        (copy,) = fetch([(w_ref.at[:, pl.ds(3 * m, m)], held)], sems)
        copy.wait()
        back = dot_nt(d_ref[...], held[...]).astype(BF)
        for i in range(c):
            out_ref[i] = back[:, i * m : (i + 1) * m]

    return call(
        body,
        1,
        [whole(n, m), HBM],
        whole(c, n, m),
        jax.ShapeDtypeStruct((c, n, m), BF),
        [pltpu.VMEM((c * m, m), BF), pltpu.SemaphoreType.DMA((1,))],
        2 * c * n * m * m,
        2 * c * m * m,
        no_table(),
        d_h,
        w,
    )


def attention_grads(a, o, dp, d_h, mates, table):
    n, width = a.shape
    m = d_h.shape[1]
    steps = table.shape[1]
    depth = width // (2 * steps)
    per = m // depth

    def body(_, a_ref, o_ref, dp_ref, dh_ref, a2_ref, o2_ref, dp2_ref, dh2_ref, out_ref, dp_all, dh_all):
        @pl.when(pl.program_id(0) == 0)
        def _():
            dp_all[:n], dp_all[n:] = dp_ref[...], dp2_ref[...]
            dh_all[:n], dh_all[n:] = dh_ref[...], dh2_ref[...]

        out_ref[:, : 3 * m] = dot_tn(jnp.concatenate([a_ref[...], a2_ref[...]]), dp_all[...]).astype(BF)
        out_ref[:, 3 * m :] = dot_tn(jnp.concatenate([o_ref[0], o2_ref[0]]), dh_all[...]).astype(BF)

    inputs = [
        pl.BlockSpec((n, depth), lambda i, t: (0, t[0, i])),
        pl.BlockSpec((1, n, depth), lambda i, t: (t[0, i] // per, 0, t[0, i] % per)),
        pl.BlockSpec((n, 3 * m), lambda i, t: (0, 0)),
        pl.BlockSpec((n, m), lambda i, t: (0, 0)),
    ]
    return call(
        body,
        steps,
        inputs * 2,
        pl.BlockSpec((depth, 4 * m), lambda i, t: (i, 0)),
        jax.ShapeDtypeStruct((steps * depth, 4 * m), BF),
        [pltpu.VMEM((2 * n, 3 * m), BF), pltpu.VMEM((2 * n, m), BF)],
        2 * n * width * 4 * m,
        width * 4 * m,
        table,
        a,
        o,
        dp,
        d_h,
        *mates,
    )


def band_list(width, c, band):
    if band % 128:
        return [slice(0, width)]
    rows = width // (c * band)
    return [slice((r * c + q) * band, (r * c + q + 1) * band) for q in range(c) for r in range(rows)]


def mlp_copies(w_ref, down_refs, held, held_down):
    gate_up = [(w_ref.at[i, :, pl.ds(0, 2)], held.at[i]) for i in range(2)]
    sources = down_refs or [w_ref.at[i, :, 2] for i in range(2)]
    return gate_up, [(source, held_down.at[i]) for i, source in enumerate(sources)]


def mlp(b, w, down, halves, band):
    n, width = b.shape
    _, c, _, w2, f = w.shape
    bands = band_list(width, c, band)

    def body(t, b_ref, w_ref, *rest):
        down_refs, (gate_ref, up_ref, m_ref, y_ref, held, held_down, turned, sems) = rest[: len(down)], rest[len(down) :]
        first, later = mlp_copies(w_ref, down_refs, held, held_down)
        copies = fetch(first + later, sems)
        at = 0
        for part in bands:
            size = part.stop - part.start
            turned[:, at : at + size] = b_ref[:, part]
            at += size
        copies[0].wait()
        gate_ref[...] = dot(turned[...], held[0].reshape(width, f))
        copies[1].wait()
        up_ref[...] = dot(turned[...], held[1].reshape(width, f))
        gate = gate_ref[...]
        m_ref[...] = (gate * jax.nn.sigmoid(gate) * up_ref[...]).astype(BF)
        for i in range(2):
            copies[2 + i].wait()
            y = dot_nt(m_ref[...], held_down[i].reshape(c * w2, f)).astype(BF)
            half = t[0, i]
            for k in range(c):
                y_ref[:, pl.ds(pl.multiple_of((2 * k + half) * w2, w2), w2)] = y[:, k * w2 : (k + 1) * w2]

    return call(
        body,
        1,
        [whole(n, width), HBM] + [HBM] * len(down),
        [whole(n, f)] * 3 + [whole(n, width)],
        [jax.ShapeDtypeStruct((n, f), F32)] * 2 + [jax.ShapeDtypeStruct((n, f), BF), jax.ShapeDtypeStruct((n, width), BF)],
        [
            pltpu.VMEM((2, c, 2, w2, f), BF),
            pltpu.VMEM((2, c, w2, f), BF),
            pltpu.VMEM((n, width), BF),
            pltpu.SemaphoreType.DMA((4,)),
        ],
        2 * n * width * 3 * f,
        2 * width * 3 * f,
        halves,
        b,
        w,
        *down,
    )


def mlp_back(dy, gate, up, w, down, halves, band):
    n, width = dy.shape
    _, c, _, w2, f = w.shape
    half = width // 2
    bands = band_list(width, c, band)

    def body(t, dy_ref, gate_ref, up_ref, w_ref, *rest):
        down_refs, (d_ref, db_ref, held, held_down, acc, sems) = rest[: len(down)], rest[len(down) :]
        later, first = mlp_copies(w_ref, down_refs, held, held_down)
        copies = fetch(first + later, sems)
        for i in range(2):
            at = t[0, i]
            ours = [dy_ref[:, pl.ds(pl.multiple_of((2 * k + at) * w2, w2), w2)] for k in range(c)]
            ours = jnp.concatenate(ours, axis=1)
            copies[i].wait()
            part = dot(ours, held_down[i].reshape(c * w2, f))
            acc[...] = part if i == 0 else acc[...] + part
        dm, gate = acc[...], gate_ref[...]
        sig = jax.nn.sigmoid(gate)
        d_ref[0] = (dm * up_ref[...] * sig * (1.0 + gate * (1.0 - sig))).astype(BF)
        d_ref[1] = (dm * gate * sig).astype(BF)
        copies[2].wait()
        copies[3].wait()
        for i in range(2):
            part = slice(i * c // 2, (i + 1) * c // 2)
            back = dot_nt(d_ref[0], held[0, part].reshape(half, f)) + dot_nt(d_ref[1], held[1, part].reshape(half, f))
            back = back.astype(BF)
            if len(bands) == 1:
                db_ref[:, i * half : (i + 1) * half] = back
            for j in range(len(bands) // 2):
                db_ref[:, bands[i * len(bands) // 2 + j]] = back[:, j * band : (j + 1) * band]

    return call(
        body,
        1,
        [whole(n, width), whole(n, f), whole(n, f), HBM] + [HBM] * len(down),
        [whole(2, n, f), whole(n, width)],
        [jax.ShapeDtypeStruct((2, n, f), BF), jax.ShapeDtypeStruct((n, width), BF)],
        [
            pltpu.VMEM((2, c, 2, w2, f), BF),
            pltpu.VMEM((2, c, w2, f), BF),
            pltpu.VMEM((n, f), F32),
            pltpu.SemaphoreType.DMA((4,)),
        ],
        2 * n * width * 3 * f,
        2 * width * 3 * f,
        halves,
        dy,
        gate,
        up,
        w,
        *down,
    )


def mlp_grads(b, d, dy, m, mates, me_s, band, merged):
    n, width = b.shape
    f = m.shape[1]
    c = lax.axis_size("col")
    depth, w2 = width // c, width // c // 2
    sizes = (depth + w2,) if merged else (depth, w2)

    def body(_, b_ref, d_ref, dy_ref, m_ref, b2_ref, d2_ref, dy2_ref, m2_ref, *rest):
        *outs, d_all, m_all = rest

        @pl.when(pl.program_id(0) == 0)
        def _():
            d_all[:n], d_all[n:] = d_ref[0], d2_ref[0]
            m_all[:n], m_all[n:] = m_ref[...], m2_ref[...]

        def rows_of(ref):
            if band % 128:
                return ref[:, pl.ds(pl.multiple_of(pl.program_id(0) * depth, depth), depth)]
            at = [pl.multiple_of((r * c + pl.program_id(0)) * band, band) for r in range(depth // band)]
            return jnp.concatenate([ref[:, pl.ds(i, band)] for i in at], axis=1)

        outs[0][0, :depth] = dot_tn(jnp.concatenate([rows_of(b_ref), rows_of(b2_ref)]), d_all[...]).astype(BF)
        start = depth if merged else 0
        outs[-1][0, start : start + w2] = dot_tn(jnp.concatenate([dy_ref[...], dy2_ref[...]]), m_all[...]).astype(BF)

    inputs = [
        pl.BlockSpec((n, width), lambda i, t: (0, 0)),
        pl.BlockSpec((1, n, f), lambda i, t: (t[0, 0], 0, 0)),
        pl.BlockSpec((n, w2), lambda i, t: (0, i * 2 + t[0, 0])),
        pl.BlockSpec((n, f), lambda i, t: (0, 0)),
    ]
    return call(
        body,
        c,
        inputs * 2,
        [pl.BlockSpec((1, size, f), lambda i, t: (i, 0, 0)) for size in sizes],
        [jax.ShapeDtypeStruct((c, size, f), BF) for size in sizes],
        [pltpu.VMEM((2 * n, f), BF)] * 2,
        2 * n * width * 3 * f,
        width * 3 * f,
        me_s.reshape(1, 1),
        b,
        d,
        dy,
        m,
        *mates,
    )


def swap(value):
    return lax.ppermute(value, "section", [(0, 1), (1, 0)])


def hop(value, axis, step):
    return lax.ppermute(value, axis, [(i, i ^ step) for i in range(lax.axis_size(axis))])


def pick(stack, index):
    return lax.dynamic_index_in_dim(stack, index, 0, keepdims=False)


def place_all(pieces, me):
    out = jnp.zeros((len(pieces), *pieces[0].shape), pieces[0].dtype)
    for k, piece in enumerate(pieces):
        out = lax.dynamic_update_index_in_dim(out, piece, me ^ k, 0)
    return out


def send_all(value, axis):
    return [value] + [hop(value, axis, k) for k in range(1, lax.axis_size(axis))]


def send_parts(stack, axis):
    me = lax.axis_index(axis)
    return [pick(stack, me)] + [hop(pick(stack, me ^ k), axis, k) for k in range(1, stack.shape[0])]


def by_place(pieces, me):
    bit = 1
    while bit < len(pieces):
        flip = (me & bit) != 0
        pieces = [jnp.where(flip, pieces[i ^ bit], pieces[i]) for i in range(len(pieces))]
        bit *= 2
    return pieces


def add_all(parts):
    out = parts[0].astype(F32)
    for part in parts[1:]:
        out = out + part.astype(F32)
    return out


def shards(
    tokens_in, out_grad, segments, positions, w_qkv, b_qkv, w_out, w_gate_up, w_down, norm_gains, norm_biases
):
    rows, cols = lax.axis_size("row"), lax.axis_size("col")
    me_s = lax.axis_index("section")
    first = me_s == 0
    seq, dc = tokens_in.shape[1:]
    width = dc * cols
    tq = seq // cols
    dr = width // rows
    fc, fr = w_gate_up.shape[3], w_down.shape[1]
    w2, v2 = dc // 2, dr // 2
    sub = rows // cols
    band = dr // cols

    def own_first(a, b):
        return jnp.where(first, a, b), jnp.where(first, b, a)

    def to_gate(x):
        if band % 128 == 0:
            return x
        return x.reshape(-1, rows, cols, band).transpose(0, 2, 1, 3).reshape(-1, width)

    def from_gate(x):
        if band % 128 == 0:
            return x
        return x.reshape(-1, cols, rows, band).transpose(0, 2, 1, 3).reshape(-1, width)

    def to_features(stack):
        return stack.transpose(1, 0, 2).reshape(stack.shape[1], width)

    def by_feature(x):
        return x.reshape(x.shape[0], cols, dc).transpose(1, 0, 2)

    me_r, me_c = lax.axis_index("row"), lax.axis_index("col")
    qo = jnp.concatenate([w_qkv[0, :, 0], w_qkv[0, :, 1], w_qkv[0, :, 2], w_out[0]], axis=1)
    qo_half = trade(qo.reshape(2, v2, 4 * dc), "section")
    qo_half, w_gate_up = tie(qo_half, w_gate_up)

    aligned = v2 % 128 == 0
    mine = 2 * jnp.arange(rows, dtype=jnp.int32) + me_s

    def gather_qo(layer):
        return lax.all_gather(qo_half[layer], ("row", "section"), axis=0, tiled=True)

    wqo0 = gather_qo(0)
    g_half = trade(w_gate_up[0].transpose(1, 0, 2), "section")

    def to_blocks(bands):
        return bands.reshape(cols, band, sub, fr).transpose(0, 2, 1, 3).reshape(rows, band, fr)

    def from_blocks(blocks):
        return blocks.reshape(cols, sub, band, fr).transpose(0, 2, 1, 3).reshape(cols, band, fc)

    def gather_mlp(*pieces):
        whole_piece = jnp.concatenate([piece.reshape(-1, fr) for piece in pieces])
        return lax.all_gather(whole_piece, ("section", "col"), axis=0, tiled=True).reshape(2, cols, -1, w2, fr)

    plain = jnp.arange(2, dtype=jnp.int32).reshape(1, 2)
    halves_of = [plain, plain ^ me_s]

    def own_and_other(parts):
        own = place_all(parts, me_c)
        return own, swap(own)

    own_tokens = pick(tokens_in, me_s)
    own_grad = pick(out_grad, me_s)
    both = jnp.stack([own_tokens, own_grad]).reshape(2, cols, tq, dc).transpose(1, 0, 2, 3)
    small = jnp.concatenate([norm_gains[0], norm_biases[0], b_qkv[0]], axis=0)
    g_half, both, small, w_down = tie(g_half, both, small, w_down)
    g_parts = send_parts(g_half[0].reshape(cols, band, fc), "col")
    d_half = trade(w_down[0].T.reshape(2, w2, fr), "section")
    small = gather(small, "section")
    wide = gather(small[:, :4], "col").transpose(1, 2, 0, 3).reshape(2, 4, width).astype(F32)
    bias = small[:, 4:].astype(F32).reshape(2, 1, 3 * dc)

    segment = pick(segments, me_s)
    position = pick(positions, me_s)
    place = jnp.arange(seq, dtype=jnp.int32)
    allowed = (segment[:, None] == segment[None, :]) & (place[None, :] <= place[:, None])
    mask = allowed.astype(F32)
    freq = jnp.power(ROPE_BASE, -2.0 * jnp.arange(ROT // 2, dtype=F32) / ROT)
    angles = position.astype(F32)[:, None] * freq[None, :]
    cosines, sines = jnp.cos(angles), jnp.sin(angles)
    rest = jnp.zeros((seq, HEAD_DIM - ROT), F32)
    none = jnp.zeros_like(sines)
    tables = jnp.stack(
        [
            jnp.concatenate([cosines, cosines, rest + 1.0] * 2, axis=1),
            jnp.concatenate([-sines, none, rest] * 2, axis=1),
            jnp.concatenate([none, sines, rest] * 2, axis=1),
        ]
    )

    tables, mask, wide, *g_parts = tie(tables, mask, wide, *g_parts)
    blocks = to_blocks(place_all(g_parts, me_c))
    blocks, both = tie(blocks, both)
    g_parts = send_parts(blocks, "row")
    late_parts = send_parts(g_half[1].reshape(cols, band, fc), "col")
    both = trade(both, "col").transpose(1, 2, 0, 3).reshape(2, tq, width)
    x = both[0].astype(F32)

    weights, kept, outputs = [], [], []
    for layer in range(2):
        g1, g2, c1, c2 = wide[layer]
        a, scaled1, inv1 = norm(x, g1, c1)
        if layer == 0:
            a, *parts = tie(a, *g_parts, *late_parts)
            wg0 = gather_mlp(place_all(parts[:rows], me_r), d_half[0])
            g_parts = send_parts(to_blocks(place_all(parts[rows:], me_c)), "row")
            down = [(), None]
        a_all = gather(a, "col").reshape(seq, width)
        a_kept = a_all
        if layer == 0:
            wqo = wqo0
        else:
            wqo = wqo1
        a_mate = swap(a_kept)
        qkv, o = attention(a_all, wqo, bias[layer], tables, mask)
        if layer == 1:
            o, grad = tie(o, both[1])
            dy_parts = send_all(grad, "row")
        o_all = gather(o, "col")
        o_kept = o_all
        o_mate = swap(o_kept)
        out = heads_out(o_all, wqo)
        if layer == 0:
            out, *g_parts = tie(out, *g_parts)
            g_piece = place_all(g_parts, me_r)
        got = trade(out.reshape(cols, tq, dc), "col")
        h = x + to_features(got).astype(F32)
        b, scaled2, inv2 = norm(h.astype(BF).astype(F32), g2, c2)
        if layer == 0:
            b, qo_half = tie(b, qo_half)
            wqo1 = gather_qo(1)
        b_all = gather(to_gate(b), "row").reshape(rows * tq, width)
        b_mate = swap(b_all)
        wg = wg0 if layer == 0 else wg1
        weights.append((wqo, wg))
        gate, up, m, partial = mlp(b_all, wg, down[layer], halves_of[layer], band)
        m_mate = swap(m)
        if layer == 0:
            gate, g_piece = tie(gate, g_piece)
            wg1 = gather_mlp(g_piece)
        else:
            gate, *parts = tie(gate, *dy_parts)
            dy_all = place_all(parts, me_r).reshape(rows * tq, width)
        partial = partial.reshape(rows, tq, width)
        if layer == 0:
            y = h + total(partial, "row")
            y, *parts = tie(y, *send_all(d_half[1], "col"))
            down[1] = own_and_other(parts)
            x = y.astype(BF).astype(F32)
            outputs.append(y)
        else:
            y_parts = send_parts(partial, "row")
        kept.append((a_kept, a_mate, scaled1, inv1, qkv, o_kept, o_mate, scaled2, inv2, b_all, b_mate, gate, up, m, m_mate))

    def to_output(pair):
        mine, theirs = own_first(*(part.astype(BF) for part in pair))
        both = jnp.stack(own_first(mine, swap(theirs)))
        parts = send_parts(both.reshape(2, tq, cols, dc).transpose(2, 0, 1, 3), "col")
        return jnp.concatenate(by_place(parts, me_c), axis=1).astype(F32)[None]

    def unshare(pair):
        return trade(jnp.stack(pair), "section")

    input_grads, qo_grads, g_grads, d_grads, norm_sums, bias_sums = ([None] * 2 for _ in range(6))
    grad = grad.astype(F32)
    for layer in (1, 0):
        g1, g2, c1, c2 = wide[layer]
        wqo, wg = weights[layer]
        a_all, a_mate, scaled1, inv1, qkv, o_all, o_mate, scaled2, inv2, b_all, b_mate, gate, up, m, m_mate = kept[layer]
        if layer == 0:
            dy_all = gather(grad.astype(BF), "row").reshape(rows * tq, width)
        dy_mate = swap(dy_all)
        d, partial = mlp_back(dy_all, gate, up, wg, down[layer], halves_of[layer], band)
        partial, d, dy_all, m, b_all = tie(partial, d, dy_all, m, b_all)
        if layer == 0:
            partial, g_piece_late = tie(partial, g_piece_late)
        got = total(partial.reshape(rows, tq, width), "row")
        mates = (b_mate, swap(d), dy_mate, m_mate)
        wide_grad, *d_wide = mlp_grads(b_all, d, dy_all, m, mates, me_s, band, layer == 1)
        got, wide_grad = tie(got, wide_grad)
        if layer == 0:
            got, placed = tie(got, to_output(outputs))
        g_piece = lax.psum_scatter(wide_grad.reshape(-1, fr), "col", scatter_dimension=0, tiled=True)
        back, gain2, shift2 = norm_back(from_gate(got), scaled2, inv2, g2)
        dh = grad + back
        dh_all = trade(by_feature(dh.astype(BF)), "col").reshape(seq, dc)
        dh_side = dh_all
        dh_mate = swap(dh_side)
        if layer == 0:
            g_late = send_parts(g_piece_late.reshape(rows, band, fr), "row")
        d_o = total(heads_back(dh_all, wqo), "col").astype(BF)
        if layer == 1:
            d_o, *parts = tie(d_o, *y_parts)
            outputs.append(h + add_all(parts))
        else:
            d_o, qo_grads[1], *g_late = tie(d_o, qo_grads[1], *g_late)
        dp, bias_sum, partial = attention_back(d_o, qkv, wqo, tables, mask)
        partial, dp = tie(partial, dp)
        got = total(partial.reshape(cols, tq, width), "col")
        if aligned:
            mates = (a_mate, o_mate, swap(dp), dh_mate)
            wide_grads = [attention_grads(a_all, o_all, dp, dh_side, mates, mine[None])]
            over = "row"
        else:
            wide_grads = [dot_tn(a_all, dp).astype(BF), dot_tn(to_features(o_all), dh_side).astype(BF)]
            over = ("row", "section")
        got, *wide_grads = tie(got, *wide_grads)
        back, gain1, shift1 = norm_back(got, scaled1, inv1, g1)
        dx = dh + back
        norm_sums[layer] = jnp.stack([gain1, gain2, shift1, shift2])
        bias_sums[layer] = bias_sum.reshape(3, dc)
        grad = dx.astype(BF).astype(F32)
        input_grads[layer] = dx
        if layer == 1:
            g_piece_late, d_grads[1] = g_piece[:dc], g_piece[dc:]
        else:
            g_late = send_parts(from_blocks(place_all(g_late, me_r)), "col")
            dx, g_piece, norm_sums = tie(dx, g_piece, norm_sums)
            g_parts = send_parts(g_piece.reshape(rows, band, fr), "row")
            sums = total(jnp.stack(norm_sums).reshape(2, 4, cols, dc).transpose(2, 0, 1, 3), "col")
            sums, *parts = tie(sums, *g_parts)
            blocks = from_blocks(place_all(parts, me_r))
            blocks, d_wide[0], *wide_grads = tie(blocks, d_wide[0], *wide_grads)
            d_parts = send_parts(d_wide[0], "col")
            g_home = trade(blocks, "col").reshape(dr, fc)
            g_home, sums, input_grads[0], *g_late = tie(g_home, sums, dx, *g_late)
            g_grads = unshare([g_home, place_all(g_late, me_c).reshape(dr, fc)])
            placed_back = to_output(input_grads)
            sums = jnp.concatenate([sums, jnp.stack(bias_sums)], axis=1)
            sums = total(add_all(send_all(sums, "row")), "section")
            g_grads, *d_parts = tie(g_grads, *d_parts)
            d_grads[0] = add_all(d_parts).astype(BF)
        pieces = [lax.psum_scatter(part, over, scatter_dimension=0, tiled=True) for part in wide_grads]
        qo_grads[layer] = jnp.concatenate(pieces, axis=1)

    qo_grads = unshare(qo_grads).reshape(dr, 4 * dc).astype(F32)
    qo_grads = [qo_grads[:, i * dc : (i + 1) * dc] for i in range(4)]
    return (
        placed,
        placed_back,
        jnp.stack(qo_grads[:3], axis=1)[None],
        sums[None, 4:],
        qo_grads[3][None],
        g_grads.astype(F32).transpose(1, 0, 2)[None],
        unshare(d_grads).astype(F32).reshape(dc, fr).T[None],
        sums[None, 0:2],
        sums[None, 2:4],
    )


def solution(mesh):
    return jax.shard_map(
        shards,
        mesh=mesh,
        in_specs=(
            P(None, "row", "col"),
            P(None, "row", "col"),
            P(None, "row"),
            P(None, "row"),
            P("section", "row", None, "col"),
            P("section", None, "col"),
            P("section", "row", "col"),
            P("section", "row", None, "col"),
            P("section", "row", "col"),
            P("section", None, "col"),
            P("section", None, "col"),
        ),
        out_specs=(
            P("section", None, "row", "col"),
            P("section", None, "row", "col"),
            P("section", "row", None, "col"),
            P("section", None, "col"),
            P("section", "row", "col"),
            P("section", "row", None, "col"),
            P("section", "row", "col"),
            P("section", None, "col"),
            P("section", None, "col"),
        ),
        check_vma=False,
    )
```

profile of v0, /device:TPU:0, one launch (start us, length us, event | category | flops | bytes accessed | tf_op | source)
XLA Modules:
  0.0 976.4 jit_solution(9994199488143637888)
XLA Ops:
  83.0 22.0 %collective-permute-done.3 = bf16[128,1408]{1,0:T(8,128)(2,1)S(1)} collective-permute-done((bf16[128,1408]{1,0:T(8,128)(2,1)}, bf16[128,1408]{1,0:T(8,128)(2,1)S(1)}, u32[]{:S(2)}, u32[]{:S(2)}) %collective-permute-start.3) | collective-permute-done | bytes 360480 | tf_op jit(solution)/shard_map/ppermute | solution.py:479
  110.1 12.0 %collective-permute-done.5 = bf16[128,1408]{1,0:T(8,128)(2,1)S(1)} collective-permute-done((bf16[128,1408]{1,0:T(8,128)(2,1)S(1)}, bf16[128,1408]{1,0:T(8,128)(2,1)S(1)}, u32[]{:S(2)}, u32[]{:S(2)}) %collective-permute-start.5) | collective-permute-done | bytes 360480 | tf_op jit(solution)/shard_map/ppermute | solution.py:479
  135.0 10.0 %all-to-all-done.5 = bf16[4,64,2048]{2,1,0:T(8,128)(2,1)S(1)} async-done(((bf16[4,64,2048]{2,1,0:T(8,128)(2,1)}), bf16[4,64,2048]{2,1,0:T(8,128)(2,1)S(1)}, u32[]{:S(2)}, u32[]{:S(2)}) %all-to-all-start.5) | async-done | bytes 1048608 | tf_op jit(solution)/shard_map/all_to_all | solution.py:19
  161.3 17.5 %collective-permute-start.10 = (bf16[128,1408]{1,0:T(8,128)(2,1)}, bf16[128,1408]{1,0:T(8,128)(2,1)S(1)}, u32[]{:S(2)}, u32[]{:S(2)}) collective-permute-start(bf16[128,1408]{1,0:T(8,128)(2,1)} %get-tuple-element.387), channel_id=1, source_target_pairs={{0,8},{4,12},{8,0},{12,4},{1,9},{5,13},{9,1},{13,5},{2,10},{6,14},... | collective-permute-start | bytes 1081352 | tf_op jit(solution)/shard_map/ppermute | solution.py:479
  189.9 12.6 %collective-permute-done.10 = bf16[128,1408]{1,0:T(8,128)(2,1)S(1)} collective-permute-done((bf16[128,1408]{1,0:T(8,128)(2,1)}, bf16[128,1408]{1,0:T(8,128)(2,1)S(1)}, u32[]{:S(2)}, u32[]{:S(2)}) %collective-permute-start.10) | collective-permute-done | bytes 360480 | tf_op jit(solution)/shard_map/ppermute | solution.py:479
  202.5 11.9 %all_to_all.151 = bf16[4,64,512]{2,1,0:T(8,128)(2,1)S(1)} all-to-all(bf16[4,64,512]{2,1,0:T(8,128)(2,1)} %bitcast.413), channel_id=1, replica_groups=mesh['section'=2,'row'=4,'col'=4] {'col'}, dimensions={0} | all-to-all | bytes 524288 | tf_op jit(solution)/shard_map/all_to_all | solution.py:19
  227.6 21.9 %all-to-all-done.8 = bf16[4,64,2048]{2,1,0:T(8,128)(2,1)S(1)} async-done(((bf16[4,64,2048]{2,1,0:T(8,128)(2,1)}), bf16[4,64,2048]{2,1,0:T(8,128)(2,1)S(1)}, u32[]{:S(2)}, u32[]{:S(2)}) %all-to-all-start.8) | async-done | bytes 1048608 | tf_op jit(solution)/shard_map/all_to_all | solution.py:19
  250.6 11.4 %shard_map.180 = (f32[256,1408]{1,0:T(8,128)}, f32[256,1408]{1,0:T(8,128)}, bf16[256,1408]{1,0:T(8,128)(2,1)}, bf16[256,2048]{1,0:T(8,128)(2,1)}) custom-call(s32[1,2]{1,0:T(1,128)} %iota.26.t, bf16[256,2048]{1,0:T(8,128)(2,1)} %bitcast.389, bf16[2,4,3,256,1408]{4,3,2,1,0:T(8,128)(2,1)} %bitcast.355), custom_call_target="tpu_custom_call" | custom-call | flops 4429185024 | bytes 17301504 | tf_op jit(solution)/shard_map/pallas_call | solution.py:63
  269.2 50.6 %all-to-all-done.10 = bf16[4,64,2048]{2,1,0:T(8,128)(2,1)S(1)} async-done(((bf16[4,64,2048]{2,1,0:T(8,128)(2,1)}), bf16[4,64,2048]{2,1,0:T(8,128)(2,1)S(1)}, u32[]{:S(2)}, u32[]{:S(2)}) %all-to-all-start.10) | async-done | bytes 1048608 | tf_op jit(solution)/shard_map/all_to_all | solution.py:19
  328.9 15.2 %all-gather.13.cloned.1.call-done = bf16[1,2048,2048]{2,1,0:T(8,128)(2,1)} async-done(((bf16[1,256,2048]{2,1,0:T(8,128)(2,1)}), bf16[1,2048,2048]{2,1,0:T(8,128)(2,1)}) %all-gather.13.cloned.1.call-update) | async-done | bytes 8388624 | tf_op jit(solution)/shard_map/all_gather | solution.py:561
  360.3 21.7 %all-to-all-done.12.o_ref = bf16[4,256,512]{2,1,0:T(8,128)(2,1)} async-done(((bf16[4,256,512]{2,1,0:T(8,128)(2,1)}), bf16[4,256,512]{2,1,0:T(8,128)(2,1)}, u32[]{:S(2)}, u32[]{:S(2)}) %all-to-all-start.12) | async-done | bytes 1048608 | tf_op jit(solution)/shard_map/all_to_all | solution.py:19
  410.4 23.4 %all-to-all-done.14 = bf16[4,64,2048]{2,1,0:T(8,128)(2,1)} async-done(((bf16[4,64,2048]{2,1,0:T(8,128)(2,1)}), bf16[4,64,2048]{2,1,0:T(8,128)(2,1)}, u32[]{:S(2)}, u32[]{:S(2)}) %all-to-all-start.14) | async-done | bytes 1048608 | tf_op jit(solution)/shard_map/all_to_all | solution.py:19
  433.8 11.5 %shard_map.183 = (f32[256,1408]{1,0:T(8,128)}, f32[256,1408]{1,0:T(8,128)}, bf16[256,1408]{1,0:T(8,128)(2,1)}, bf16[256,2048]{1,0:T(8,128)(2,1)}) custom-call(s32[1,2]{1,0:T(1,128)} %iota_xor_fusion.t, bf16[256,2048]{1,0:T(8,128)(2,1)} %bitcast.74.b_ref, bf16[2,4,2,256,1408]{4,3,2,1,0:T(8,128)(2,1)} %bitcast.357, bf16[4,256,1408]{2,1,0:T(8,128)(2,1)} %copy-done, ...), custom_call_target="tpu_custom_call" | custom-call | flops 4429185024 | bytes 17301504 | tf_op jit(solution)/shard_map/pallas_call | solution.py:63
  452.9 13.2 %shard_map.184 = (bf16[2,256,1408]{2,1,0:T(8,128)(2,1)}, bf16[256,2048]{1,0:T(8,128)(2,1)}) custom-call(s32[1,2]{1,0:T(1,128)} %iota_xor_fusion.t, bf16[256,2048]{1,0:T(8,128)(2,1)} %bitcast.365, f32[256,1408]{1,0:T(8,128)} %get-tuple-element.187.gate_ref, f32[256,1408]{1,0:T(8,128)} %get-tuple-element.188.up_ref, bf16[2,4,2,256,1408]{4,3,2,1,0:T(8,128)(2,1)} %bitcast.358, ...), custom_call_target="tpu_custom_call" | custom-call | flops 4429185024 | bytes 17301504 | tf_op jit(solution)/shard_map/pallas_call | solution.py:63
  466.2 9.6 all-to-all-start.15
  482.5 10.0 %shard_map.185 = bf16[4,768,1408]{2,1,0:T(8,128)(2,1)} custom-call(s32[1,1]{1,0:T(1,128)} %bitcast.91._, bf16[256,2048]{1,0:T(8,128)(2,1)} %bitcast.74.b_ref, bf16[2,256,1408]{2,1,0:T(8,128)(2,1)} %get-tuple-element.194.d_ref, bf16[256,2048]{1,0:T(8,128)(2,1)} %bitcast.366, bf16[256,1408]{1,0:T(8,128)(2,1)} %get-tuple-element.196.m_ref, ...), custom_call_target="tpu_custom_call" | custom-call | flops 4429185024 | bytes 8650752 | tf_op jit(solution)/shard_map/pallas_call | solution.py:63
  492.5 9.5 all-to-all-done.15
  504.4 12.1 %all_to_all.152 = bf16[4,64,512]{2,1,0:T(8,128)(2,1)} all-to-all(bf16[4,64,512]{2,1,0:T(8,128)(2,1)S(1)} %copy.129), channel_id=1, replica_groups=mesh['section'=2,'row'=4,'col'=4] {'col'}, dimensions={0} | all-to-all | bytes 524288 | tf_op jit(solution)/shard_map/all_to_all | solution.py:19
  529.5 20.1 %all-to-all-done.17 = bf16[4,256,512]{2,1,0:T(8,128)(2,1)S(1)} async-done(((bf16[4,256,512]{2,1,0:T(8,128)(2,1)}), bf16[4,256,512]{2,1,0:T(8,128)(2,1)S(1)}, u32[]{:S(2)}, u32[]{:S(2)}) %all-to-all-start.17) | async-done | bytes 1048608 | tf_op jit(solution)/shard_map/all_to_all | solution.py:19
  551.3 9.2 shard_map.187
  565.5 15.2 %all-to-all-done.18 = bf16[4,64,2048]{2,1,0:T(8,128)(2,1)S(1)} async-done(((bf16[4,64,2048]{2,1,0:T(8,128)(2,1)}), bf16[4,64,2048]{2,1,0:T(8,128)(2,1)S(1)}, u32[]{:S(2)}, u32[]{:S(2)}) %all-to-all-start.18) | async-done | bytes 1048608 | tf_op jit(solution)/shard_map/all_to_all | solution.py:19
  590.7 28.7 %all_to_all.153 = bf16[4,64,2048]{2,1,0:T(8,128)(2,1)} all-to-all(bf16[4,64,2048]{2,1,0:T(8,128)(2,1)S(1)} %broadcast_in_dim.239), channel_id=1, replica_groups=mesh['section'=2,'row'=4,'col'=4] {'row'}, dimensions={0} | all-to-all | bytes 2097152 | tf_op jit(solution)/shard_map/all_to_all | solution.py:19
  619.9 13.5 %shard_map.189 = (bf16[2,256,1408]{2,1,0:T(8,128)(2,1)}, bf16[256,2048]{1,0:T(8,128)(2,1)}) custom-call(s32[1,2]{1,0:T(1,128)} %iota.24.t, bf16[256,2048]{1,0:T(8,128)(2,1)} %bitcast.386, f32[256,1408]{1,0:T(8,128)} %get-tuple-element.206.gate_ref, f32[256,1408]{1,0:T(8,128)} %get-tuple-element.207.up_ref, bf16[2,4,3,256,1408]{4,3,2,1,0:T(8,128)(2,1)} %bitcast.356), custom_call_target="tpu_custom_call" | custom-call | flops 4429185024 | bytes 17301504 | tf_op jit(solution)/shard_map/pallas_call | solution.py:63
  646.6 9.6 shard_map.190
  656.2 36.1 %all-to-all-done.20 = bf16[4,64,2048]{2,1,0:T(8,128)(2,1)S(1)} async-done(((bf16[4,64,2048]{2,1,0:T(8,128)(2,1)}), bf16[4,64,2048]{2,1,0:T(8,128)(2,1)S(1)}, u32[]{:S(2)}, u32[]{:S(2)}) %all-to-all-start.20) | async-done | bytes 1048608 | tf_op jit(solution)/shard_map/all_to_all | solution.py:19
  708.9 9.3 all_to_all.154
  736.4 16.2 %all-to-all-done.22 = bf16[4,256,512]{2,1,0:T(8,128)(2,1)} async-done(((bf16[4,256,512]{2,1,0:T(8,128)(2,1)}), bf16[4,256,512]{2,1,0:T(8,128)(2,1)}, u32[]{:S(2)}, u32[]{:S(2)}) %all-to-all-start.22) | async-done | bytes 1048608 | tf_op jit(solution)/shard_map/all_to_all | solution.py:19
  760.8 9.3 shard_map.192
  778.3 22.5 %all-to-all-done.23 = bf16[4,64,2048]{2,1,0:T(8,128)(2,1)} async-done(((bf16[4,64,2048]{2,1,0:T(8,128)(2,1)}), bf16[4,64,2048]{2,1,0:T(8,128)(2,1)}, u32[]{:S(2)}, u32[]{:S(2)}) %all-to-all-start.23) | async-done | bytes 1048608 | tf_op jit(solution)/shard_map/all_to_all | solution.py:19
  833.1 12.2 %collective-permute-done.46 = bf16[128,1408]{1,0:T(8,128)(2,1)S(1)} collective-permute-done((bf16[128,1408]{1,0:T(8,128)(2,1)S(1)}, bf16[128,1408]{1,0:T(8,128)(2,1)S(1)}, u32[]{:S(2)}, u32[]{:S(2)}) %collective-permute-start.46) | collective-permute-done | bytes 360480 | tf_op jit(solution)/shard_map/ppermute | solution.py:479
  869.6 12.3 %collective-permute-done.48 = bf16[128,1408]{1,0:T(8,128)(2,1)S(1)} collective-permute-done((bf16[128,1408]{1,0:T(8,128)(2,1)S(1)}, bf16[128,1408]{1,0:T(8,128)(2,1)S(1)}, u32[]{:S(2)}, u32[]{:S(2)}) %collective-permute-start.48) | collective-permute-done | bytes 360480 | tf_op jit(solution)/shard_map/ppermute | solution.py:479
  933.4 9.6 copy.138
  (557 shorter events, 439.9 us)
Async XLA Ops:
  7.2 137.8 %all-gather.11.cloned.1.call-start = ((), (), s32[]{:S(2)}) async-start(), calls=%async_computation.40 | async-start | bytes 9437184 | tf_op jit(solution)/shard_map/all_gather | solution.py:561
  39.2 39.9 %collective-permute-start.6 = (bf16[128,1408]{1,0:T(8,128)(2,1)}, bf16[128,1408]{1,0:T(8,128)(2,1)}, u32[]{:S(2)}, u32[]{:S(2)}) collective-permute-start(bf16[128,1408]{1,0:T(8,128)(2,1)} %get-tuple-element.392), channel_id=1, source_target_pairs={{0,1},{1,0},{2,3},{3,2},{4,5},{5,4},{6,7},{7,6},{8,9},{9,8},{10,11... | collective-permute-start | bytes 1081352 | tf_op jit(solution)/shard_map/ppermute | solution.py:479
  41.1 41.8 %collective-permute-start.7 = (bf16[128,1408]{1,0:T(8,128)(2,1)}, bf16[128,1408]{1,0:T(8,128)(2,1)}, u32[]{:S(2)}, u32[]{:S(2)}) collective-permute-start(bf16[128,1408]{1,0:T(8,128)(2,1)} %get-tuple-element.391), channel_id=1, source_target_pairs={{0,2},{1,3},{2,0},{3,1},{4,6},{5,7},{6,4},{7,5},{8,10},{9,11},{10,... | collective-permute-start | bytes 1081352 | tf_op jit(solution)/shard_map/ppermute | solution.py:479
  69.4 180.2 %all-gather.7.cloned.1.call-start = ((), (), s32[]{:S(2)}) async-start(), calls=%async_computation.34 | async-start | bytes 19464192 | tf_op jit(solution)/shard_map/all_gather | solution.py:574
  71.9 38.2 %collective-permute-start.4 = (bf16[128,1408]{1,0:T(8,128)(2,1)}, bf16[128,1408]{1,0:T(8,128)(2,1)}, u32[]{:S(2)}, u32[]{:S(2)}) collective-permute-start(bf16[128,1408]{1,0:T(8,128)(2,1)} %get-tuple-element.395), channel_id=1, source_target_pairs={{0,8},{4,12},{8,0},{12,4},{1,9},{5,13},{9,1},{13,5},{2,10},{6,14},... | collective-permute-start | bytes 1081352 | tf_op jit(solution)/shard_map/ppermute | solution.py:479
  79.1 43.0 %collective-permute-start.5 = (bf16[128,1408]{1,0:T(8,128)(2,1)S(1)}, bf16[128,1408]{1,0:T(8,128)(2,1)S(1)}, u32[]{:S(2)}, u32[]{:S(2)}) collective-permute-start(bf16[128,1408]{1,0:T(8,128)(2,1)S(1)} %get-tuple-element.394), channel_id=1, source_target_pairs={{0,12},{4,8},{8,4},{12,0},{1,13},{5,9},{9,5},{13,1},{2,14},{6,10},... | collective-permute-start | bytes 1081352 | tf_op jit(solution)/shard_map/ppermute | solution.py:479
  159.1 185.0 %all-gather.13.cloned.1.call-start = ((), (), s32[]{:S(2)}) async-start(), calls=%async_computation.41 | async-start | bytes 9437184 | tf_op jit(solution)/shard_map/all_gather | solution.py:561
  161.3 41.2 %collective-permute-start.10 = (bf16[128,1408]{1,0:T(8,128)(2,1)}, bf16[128,1408]{1,0:T(8,128)(2,1)S(1)}, u32[]{:S(2)}, u32[]{:S(2)}) collective-permute-start(bf16[128,1408]{1,0:T(8,128)(2,1)} %get-tuple-element.387), channel_id=1, source_target_pairs={{0,8},{4,12},{8,0},{12,4},{1,9},{5,13},{9,1},{13,5},{2,10},{6,14},... | collective-permute-start | bytes 1081352 | tf_op jit(solution)/shard_map/ppermute | solution.py:479
  226.3 207.4 %all-gather.9.cloned.1.call-start = ((), (), s32[]{:S(2)}) async-start(), calls=%async_computation.35 | async-start | bytes 12976128 | tf_op jit(solution)/shard_map/all_gather | solution.py:574
  262.0 57.9 %all-to-all-start.10 = ((bf16[4,64,2048]{2,1,0:T(8,128)(2,1)}), bf16[4,64,2048]{2,1,0:T(8,128)(2,1)S(1)}, u32[]{:S(2)}, u32[]{:S(2)}) async-start(bf16[4,64,2048]{2,1,0:T(8,128)(2,1)} %bitcast.417), calls=%async_computation.10 | async-start | bytes 2097152 | tf_op jit(solution)/shard_map/all_to_all | solution.py:19
  265.7 54.4 %collective-permute-start.12 = (bf16[256,1408]{1,0:T(8,128)(2,1)S(1)}, bf16[256,1408]{1,0:T(8,128)(2,1)}, u32[]{:S(2)}, u32[]{:S(2)}) collective-permute-start(bf16[256,1408]{1,0:T(8,128)(2,1)S(1)} %copy-done.20), channel_id=1, source_target_pairs={{0,1},{1,0},{2,3},{3,2},{4,5},{5,4},{6,7},{7,6},{8,9},{9,8},{10,11... | collective-permute-start | bytes 2162696 | tf_op jit(solution)/shard_map/ppermute | solution.py:479
  267.1 53.0 %collective-permute-start.13 = (bf16[256,1408]{1,0:T(8,128)(2,1)S(1)}, bf16[256,1408]{1,0:T(8,128)(2,1)}, u32[]{:S(2)}, u32[]{:S(2)}) collective-permute-start(bf16[256,1408]{1,0:T(8,128)(2,1)S(1)} %copy-done.20), channel_id=1, source_target_pairs={{0,2},{1,3},{2,0},{3,1},{4,6},{5,7},{6,4},{7,5},{8,10},{9,11},{10,... | collective-permute-start | bytes 2162696 | tf_op jit(solution)/shard_map/ppermute | solution.py:479
  267.5 52.5 %collective-permute-start.14 = (bf16[256,1408]{1,0:T(8,128)(2,1)S(1)}, bf16[256,1408]{1,0:T(8,128)(2,1)S(1)}, u32[]{:S(2)}, u32[]{:S(2)}) collective-permute-start(bf16[256,1408]{1,0:T(8,128)(2,1)S(1)} %copy-done.20), channel_id=1, source_target_pairs={{0,3},{1,2},{2,1},{3,0},{4,7},{5,6},{6,5},{7,4},{8,11},{9,10},{10,... | collective-permute-start | bytes 2162696 | tf_op jit(solution)/shard_map/ppermute | solution.py:479
  406.0 39.3 %collective-permute-start.16 = (bf16[64,2048]{1,0:T(8,128)(2,1)}, bf16[64,2048]{1,0:T(8,128)(2,1)}, u32[]{:S(2)}, u32[]{:S(2)}) collective-permute-start(bf16[64,2048]{1,0:T(8,128)(2,1)} %bitcast.393), channel_id=1, source_target_pairs={{0,4},{4,0},{8,12},{12,8},{1,5},{5,1},{9,13},{13,9},{2,6},{6,2},{1... | collective-permute-start | bytes 786440 | tf_op jit(solution)/shard_map/ppermute | solution.py:479
  408.0 40.8 %collective-permute-start.17 = (bf16[64,2048]{1,0:T(8,128)(2,1)}, bf16[64,2048]{1,0:T(8,128)(2,1)}, u32[]{:S(2)}, u32[]{:S(2)}) collective-permute-start(bf16[64,2048]{1,0:T(8,128)(2,1)} %bitcast.394), channel_id=1, source_target_pairs={{0,8},{4,12},{8,0},{12,4},{1,9},{5,13},{9,1},{13,5},{2,10},{6,14},... | collective-permute-start | bytes 786440 | tf_op jit(solution)/shard_map/ppermute | solution.py:479
  410.4 38.4 %collective-permute-start.18 = (bf16[64,2048]{1,0:T(8,128)(2,1)}, bf16[64,2048]{1,0:T(8,128)(2,1)}, u32[]{:S(2)}, u32[]{:S(2)}) collective-permute-start(bf16[64,2048]{1,0:T(8,128)(2,1)} %bitcast.395), channel_id=1, source_target_pairs={{0,12},{4,8},{8,4},{12,0},{1,13},{5,9},{9,5},{13,1},{2,14},{6,10},... | collective-permute-start | bytes 786440 | tf_op jit(solution)/shard_map/ppermute | solution.py:479
  475.8 157.7 %reduce-scatter.5.cloned.1.call-start = ((), (), s32[]{:S(2)}) async-start(), calls=%async_computation.36 | async-start | bytes 10813440 | tf_op jit(solution)/shard_map/reduce_scatter | solution.py:704
  529.0 51.9 %collective-permute-start.26 = (bf16[256,2048]{1,0:T(8,128)(2,1)}, bf16[256,2048]{1,0:T(8,128)(2,1)}, u32[]{:S(2)}, u32[]{:S(2)}) collective-permute-start(bf16[256,2048]{1,0:T(8,128)(2,1)} %bitcast.68.a_ref), channel_id=1, source_target_pairs={{0,16},{16,0},{1,17},{17,1},{2,18},{18,2},{3,19},{19,3},{4,20},{20... | collective-permute-start | bytes 3145736 | tf_op jit(solution)/shard_map/ppermute | solution.py:475
  529.0 51.9 %collective-permute-start.27 = (bf16[4,256,512]{2,1,0:T(8,128)(2,1)}, bf16[4,256,512]{2,1,0:T(8,128)(2,1)}, u32[]{:S(2)}, u32[]{:S(2)}) collective-permute-start(bf16[4,256,512]{2,1,0:T(8,128)(2,1)} %all-to-all-done.12.o_ref), channel_id=1, source_target_pairs={{0,16},{16,0},{1,17},{17,1},{2,18},{18,2},{3,19},{19,3},{4,20},{20... | collective-permute-start | bytes 3145736 | tf_op jit(solution)/shard_map/ppermute | solution.py:475
  564.2 190.5 %reduce-scatter.7.cloned.1.call-start = ((), (), s32[]{:S(2)}) async-start(), calls=%async_computation.37 | async-start | bytes 5242880 | tf_op jit(solution)/shard_map/reduce_scatter | solution.py:754
  636.1 56.2 %all-to-all-start.20 = ((bf16[4,64,2048]{2,1,0:T(8,128)(2,1)}), bf16[4,64,2048]{2,1,0:T(8,128)(2,1)S(1)}, u32[]{:S(2)}, u32[]{:S(2)}) async-start(bf16[4,64,2048]{2,1,0:T(8,128)(2,1)} %bitcast.415), calls=%async_computation.21 | async-start | bytes 2097152 | tf_op jit(solution)/shard_map/all_to_all | solution.py:19
  639.8 172.4 %reduce-scatter.9.cloned.1.call-start = ((), (), s32[]{:S(2)}) async-start(), calls=%async_computation.38 | async-start | bytes 7208960 | tf_op jit(solution)/shard_map/reduce_scatter | solution.py:704
  735.8 67.3 %collective-permute-start.41 = (bf16[256,2048]{1,0:T(8,128)(2,1)S(1)}, bf16[256,2048]{1,0:T(8,128)(2,1)}, u32[]{:S(2)}, u32[]{:S(2)}) collective-permute-start(bf16[256,2048]{1,0:T(8,128)(2,1)S(1)} %bitcast.370), channel_id=1, source_target_pairs={{0,16},{16,0},{1,17},{17,1},{2,18},{18,2},{3,19},{19,3},{4,20},{20... | collective-permute-start | bytes 3145736 | tf_op jit(solution)/shard_map/ppermute | solution.py:475
  735.8 67.3 %collective-permute-start.42 = (bf16[4,256,512]{2,1,0:T(8,128)(2,1)S(1)}, bf16[4,256,512]{2,1,0:T(8,128)(2,1)}, u32[]{:S(2)}, u32[]{:S(2)}) collective-permute-start(bf16[4,256,512]{2,1,0:T(8,128)(2,1)S(1)} %copy-done.6), channel_id=1, source_target_pairs={{0,16},{16,0},{1,17},{17,1},{2,18},{18,2},{3,19},{19,3},{4,20},{20... | collective-permute-start | bytes 3145736 | tf_op jit(solution)/shard_map/ppermute | solution.py:475
  754.8 48.3 %collective-permute-start.44 = (bf16[256,512]{1,0:T(8,128)(2,1)S(1)}, bf16[256,512]{1,0:T(8,128)(2,1)}, u32[]{:S(2)}, u32[]{:S(2)}) collective-permute-start(bf16[256,512]{1,0:T(8,128)(2,1)S(1)} %bitcast.400), channel_id=1, source_target_pairs={{0,16},{16,0},{1,17},{17,1},{2,18},{18,2},{3,19},{19,3},{4,20},{20... | collective-permute-start | bytes 786440 | tf_op jit(solution)/shard_map/ppermute | solution.py:475
  824.0 134.1 %reduce-scatter.11.cloned.1.call-start = ((), (), s32[]{:S(2)}) async-start(), calls=%async_computation.39 | async-start | bytes 5242880 | tf_op jit(solution)/shard_map/reduce_scatter | solution.py:754
  851.3 39.3 %all-to-all-start.25 = ((bf16[4,128,1408]{2,1,0:T(8,128)(2,1)}), bf16[4,128,1408]{2,1,0:T(8,128)(2,1)S(1)}, u32[]{:S(2)}, u32[]{:S(2)}) async-start(bf16[4,128,1408]{2,1,0:T(8,128)(2,1)} %bitcast_dynamic-update-slice_fusion.12), calls=%async_computation.28 | async-start | bytes 2883584 | tf_op jit(solution)/shard_map/all_to_all | solution.py:19
  866.2 42.3 %collective-permute-start.58 = (bf16[256,1408]{1,0:T(8,128)(2,1)}, bf16[256,1408]{1,0:T(8,128)(2,1)}, u32[]{:S(2)}, u32[]{:S(2)}) collective-permute-start(bf16[256,1408]{1,0:T(8,128)(2,1)} %get-tuple-element.365), channel_id=1, source_target_pairs={{0,1},{1,0},{2,3},{3,2},{4,5},{5,4},{6,7},{7,6},{8,9},{9,8},{10,11... | collective-permute-start | bytes 2162696 | tf_op jit(solution)/shard_map/ppermute | solution.py:479
  868.1 41.9 %collective-permute-start.59 = (bf16[256,1408]{1,0:T(8,128)(2,1)}, bf16[256,1408]{1,0:T(8,128)(2,1)}, u32[]{:S(2)}, u32[]{:S(2)}) collective-permute-start(bf16[256,1408]{1,0:T(8,128)(2,1)} %get-tuple-element.364), channel_id=1, source_target_pairs={{0,2},{1,3},{2,0},{3,1},{4,6},{5,7},{6,4},{7,5},{8,10},{9,11},{10,... | collective-permute-start | bytes 2162696 | tf_op jit(solution)/shard_map/ppermute | solution.py:479
  881.9 36.2 %collective-permute-start.60 = (bf16[256,1408]{1,0:T(8,128)(2,1)}, bf16[256,1408]{1,0:T(8,128)(2,1)}, u32[]{:S(2)}, u32[]{:S(2)}) collective-permute-start(bf16[256,1408]{1,0:T(8,128)(2,1)} %get-tuple-element.363), channel_id=1, source_target_pairs={{0,3},{1,2},{2,1},{3,0},{4,7},{5,6},{6,5},{7,4},{8,11},{9,10},{10,... | collective-permute-start | bytes 2162696 | tf_op jit(solution)/shard_map/ppermute | solution.py:479
  891.2 51.9 %collective-permute-start.55 = (f32[2,7,512]{2,1,0:T(8,128)}, f32[2,7,512]{2,1,0:T(8,128)S(1)}, u32[]{:S(2)}, u32[]{:S(2)}) collective-permute-start(f32[2,7,512]{2,1,0:T(8,128)} %maximum_maximum_fusion), channel_id=1, source_target_pairs={{0,4},{4,0},{8,12},{12,8},{1,5},{5,1},{9,13},{13,9},{2,6},{6,2},{1... | collective-permute-start | bytes 86024 | tf_op jit(solution)/shard_map/ppermute | solution.py:479
  898.3 44.9 %collective-permute-start.56 = (f32[2,7,512]{2,1,0:T(8,128)}, f32[2,7,512]{2,1,0:T(8,128)S(1)}, u32[]{:S(2)}, u32[]{:S(2)}) collective-permute-start(f32[2,7,512]{2,1,0:T(8,128)} %maximum_maximum_fusion), channel_id=1, source_target_pairs={{0,8},{4,12},{8,0},{12,4},{1,9},{5,13},{9,1},{13,5},{2,10},{6,14},... | collective-permute-start | bytes 86024 | tf_op jit(solution)/shard_map/ppermute | solution.py:479
  (146 other events, 1863.4 us)
Sparse Core Ops, SparseCore 0:
  17.0 113.3 all-gather.10
  132.8 105.2 all-gather.6
  239.7 104.2 all-gather.12
  345.8 80.1 all-gather.8
  502.4 110.0 reduce-scatter.4
  614.6 93.6 reduce-scatter.6
  712.0 92.9 reduce-scatter.8
  849.7 83.5 reduce-scatter.10
where the time goes:
time: 994 us; the launch traced here: 976 us
  waiting for transfers between devices  408 us (41%)
  starting transfers between devices  187 us (19%)
  Pallas kernels  136 us (14%)
  local copies, waits for them, and re-layouts  110 us (11%)
  blocking collectives  81.5 us (8%)
  other arithmetic  37.6 us (4%)
  between operations  16.4 us (2%)
    all_to_all x22, waiting for transfers between devices, trade(): return lax.all_to_all(stack, axis, split_axis=0, concat_axis=0)  266 us
    pallas_call x16, Pallas kernels, call(): pl.pallas_call(body, grid_spec=pltpu.PrefetchScalarGridSpec(num_scalar_pr...  136 us
    ppermute x42, waiting for transfers between devices, hop(): lax.ppermute(value, axis, [(i, i ^ step) for i in range(lax.axis_size(axi...  116 us
    all_to_all x22, starting transfers between devices, trade(): return lax.all_to_all(stack, axis, split_axis=0, concat_axis=0)  93.4 us
    ppermute x42, starting transfers between devices, hop(): lax.ppermute(value, axis, [(i, i ^ step) for i in range(lax.axis_size(axi...  90 us
    all_to_all x8, blocking collectives, trade(): return lax.all_to_all(stack, axis, split_axis=0, concat_axis=0)  81.5 us
    unnamed x183, local copies, waits for them, and re-layouts  29.6 us
    dynamic_update_slice x36, local copies, waits for them, and re-layouts, place_all(): out = lax.dynamic_update_index_in_dim(out, piece, me ^ k, 0)  26.4 us
  transfers between devices with their start and end apart: 91, of which 39 were waited for; matrix products, arithmetic and copies ran while one was open for 12% of the time, Pallas kernels for 13%

commit v1 on v0

--- a/solution.py
+++ b/solution.py
@@ -644,6 +644,9 @@
         if layer == 0:
             out, *g_parts = tie(out, *g_parts)
             g_piece = place_all(g_parts, me_r)
+        if layer == 1:
+            out, *parts = tie(out, *dy_parts)
+            dy_all = place_all(parts, me_r).reshape(rows * tq, width)
         got = trade(out.reshape(cols, tq, dc), "col")
         h = x + to_features(got).astype(F32)
         b, scaled2, inv2 = norm(h.astype(BF).astype(F32), g2, c2)
@@ -659,9 +662,6 @@
         if layer == 0:
             gate, g_piece = tie(gate, g_piece)
             wg1 = gather_mlp(g_piece)
-        else:
-            gate, *parts = tie(gate, *dy_parts)
-            dy_all = place_all(parts, me_r).reshape(rows * tq, width)
         partial = partial.reshape(rows, tq, width)
         if layer == 0:
             y = h + total(partial, "row")
@@ -699,8 +699,6 @@
         mates = (b_mate, swap(d), dy_mate, m_mate)
         wide_grad, *d_wide = mlp_grads(b_all, d, dy_all, m, mates, me_s, band, layer == 1)
         got, wide_grad = tie(got, wide_grad)
-        if layer == 0:
-            got, placed = tie(got, to_output(outputs))
         g_piece = lax.psum_scatter(wide_grad.reshape(-1, fr), "col", scatter_dimension=0, tiled=True)
         back, gain2, shift2 = norm_back(from_gate(got), scaled2, inv2, g2)
         dh = grad + back
@@ -714,7 +712,7 @@
             d_o, *parts = tie(d_o, *y_parts)
             outputs.append(h + add_all(parts))
         else:
-            d_o, qo_grads[1], *g_late = tie(d_o, qo_grads[1], *g_late)
+            d_o, qo_grads[1], placed, *g_late = tie(d_o, qo_grads[1], to_output(outputs), *g_late)
         dp, bias_sum, partial = attention_back(d_o, qkv, wqo, tables, mask)
         partial, dp = tie(partial, dp)
         got = total(partial.reshape(cols, tq, width), "col")
@@ -739,12 +737,13 @@
             dx, g_piece, norm_sums = tie(dx, g_piece, norm_sums)
             g_parts = send_parts(g_piece.reshape(rows, band, fr), "row")
             sums = total(jnp.stack(norm_sums).reshape(2, 4, cols, dc).transpose(2, 0, 1, 3), "col")
-            sums, *parts = tie(sums, *g_parts)
-            blocks = from_blocks(place_all(parts, me_r))
+            sums, *parts = tie(sums, *g_parts, *g_late)
+            g_late = parts[rows:]
+            blocks = from_blocks(place_all(parts[:rows], me_r))
             blocks, d_wide[0], *wide_grads = tie(blocks, d_wide[0], *wide_grads)
             d_parts = send_parts(d_wide[0], "col")
             g_home = trade(blocks, "col").reshape(dr, fc)
-            g_home, sums, input_grads[0], *g_late = tie(g_home, sums, dx, *g_late)
+            g_home, sums, input_grads[0] = tie(g_home, sums, dx)
             g_grads = unshare([g_home, place_all(g_late, me_c).reshape(dr, fc)])
             placed_back = to_output(input_grads)
             sums = jnp.concatenate([sums, jnp.stack(bias_sums)], axis=1)

time: 994 us -> 962 us (0.968)
  waiting for transfers between devices: 408 us -> 377 us
    ppermute x42, waiting for transfers between devices: 116 us -> 95.9 us  [hop(): lax.ppermute(value, axis, [(i, i ^ step) for i in range(lax.axis_size(axi...]
    all_to_all x22, waiting for transfers between devices: 266 us -> 253 us  [trade(): return lax.all_to_all(stack, axis, split_axis=0, concat_axis=0)]
    unnamed x183 -> x173, local copies, waits for them, and re-layouts: 29.6 us -> 28.6 us
  transfers between devices with their start and end apart: 91 -> 91, of which waited for: 39 -> 37; matrix products, arithmetic and copies ran while one was open for 12% -> 12% of each run, Pallas kernels for 13% -> 12%
where the time goes in v1:
time: 962 us; the launch traced here: 944 us
  waiting for transfers between devices  377 us (39%)
  starting transfers between devices  185 us (19%)
  Pallas kernels  137 us (14%)
  local copies, waits for them, and re-layouts  112 us (12%)
  blocking collectives  79.7 us (8%)
  other arithmetic  37.2 us (4%)
  between operations  16.3 us (2%)
    all_to_all x22, waiting for transfers between devices, trade(): return lax.all_to_all(stack, axis, split_axis=0, concat_axis=0)  253 us
    pallas_call x16, Pallas kernels, call(): pl.pallas_call(body, grid_spec=pltpu.PrefetchScalarGridSpec(num_scalar_pr...  137 us
    ppermute x42, waiting for transfers between devices, hop(): lax.ppermute(value, axis, [(i, i ^ step) for i in range(lax.axis_size(axi...  95.9 us
    ppermute x42, starting transfers between devices, hop(): lax.ppermute(value, axis, [(i, i ^ step) for i in range(lax.axis_size(axi...  93.1 us
    all_to_all x22, starting transfers between devices, trade(): return lax.all_to_all(stack, axis, split_axis=0, concat_axis=0)  87.8 us
    all_to_all x8, blocking collectives, trade(): return lax.all_to_all(stack, axis, split_axis=0, concat_axis=0)  79.7 us
    unnamed x173, local copies, waits for them, and re-layouts  28.6 us
    dynamic_update_slice x36, local copies, waits for them, and re-layouts, place_all(): out = lax.dynamic_update_index_in_dim(out, piece, me ^ k, 0)  27.2 us
  transfers between devices with their start and end apart: 91, of which 37 were waited for; matrix products, arithmetic and copies ran while one was open for 12% of the time, Pallas kernels for 12%

profile of v1, /device:TPU:0, one launch (start us, length us, event | category | flops | bytes accessed | tf_op | source)
XLA Modules:
  0.0 943.9 jit_solution(6862949085112447489)
XLA Ops:
  83.1 22.0 %collective-permute-done.3 = bf16[128,1408]{1,0:T(8,128)(2,1)S(1)} collective-permute-done((bf16[128,1408]{1,0:T(8,128)(2,1)}, bf16[128,1408]{1,0:T(8,128)(2,1)S(1)}, u32[]{:S(2)}, u32[]{:S(2)}) %collective-permute-start.3) | collective-permute-done | bytes 360480 | tf_op jit(solution)/shard_map/ppermute | solution.py:479
  110.2 12.0 %collective-permute-done.5 = bf16[128,1408]{1,0:T(8,128)(2,1)S(1)} collective-permute-done((bf16[128,1408]{1,0:T(8,128)(2,1)S(1)}, bf16[128,1408]{1,0:T(8,128)(2,1)S(1)}, u32[]{:S(2)}, u32[]{:S(2)}) %collective-permute-start.5) | collective-permute-done | bytes 360480 | tf_op jit(solution)/shard_map/ppermute | solution.py:479
  135.0 10.1 %all-to-all-done.5 = bf16[4,64,2048]{2,1,0:T(8,128)(2,1)S(1)} async-done(((bf16[4,64,2048]{2,1,0:T(8,128)(2,1)}), bf16[4,64,2048]{2,1,0:T(8,128)(2,1)S(1)}, u32[]{:S(2)}, u32[]{:S(2)}) %all-to-all-start.5) | async-done | bytes 1048608 | tf_op jit(solution)/shard_map/all_to_all | solution.py:19
  161.4 17.4 %collective-permute-start.10 = (bf16[128,1408]{1,0:T(8,128)(2,1)}, bf16[128,1408]{1,0:T(8,128)(2,1)S(1)}, u32[]{:S(2)}, u32[]{:S(2)}) collective-permute-start(bf16[128,1408]{1,0:T(8,128)(2,1)} %get-tuple-element.385), channel_id=1, source_target_pairs={{0,8},{4,12},{8,0},{12,4},{1,9},{5,13},{9,1},{13,5},{2,10},{6,14},... | collective-permute-start | bytes 1081352 | tf_op jit(solution)/shard_map/ppermute | solution.py:479
  189.9 12.6 %collective-permute-done.10 = bf16[128,1408]{1,0:T(8,128)(2,1)S(1)} collective-permute-done((bf16[128,1408]{1,0:T(8,128)(2,1)}, bf16[128,1408]{1,0:T(8,128)(2,1)S(1)}, u32[]{:S(2)}, u32[]{:S(2)}) %collective-permute-start.10) | collective-permute-done | bytes 360480 | tf_op jit(solution)/shard_map/ppermute | solution.py:479
  202.5 11.9 %all_to_all.151 = bf16[4,64,512]{2,1,0:T(8,128)(2,1)S(1)} all-to-all(bf16[4,64,512]{2,1,0:T(8,128)(2,1)} %bitcast.411), channel_id=1, replica_groups=mesh['section'=2,'row'=4,'col'=4] {'col'}, dimensions={0} | all-to-all | bytes 524288 | tf_op jit(solution)/shard_map/all_to_all | solution.py:19
  227.7 22.0 %all-to-all-done.8 = bf16[4,64,2048]{2,1,0:T(8,128)(2,1)S(1)} async-done(((bf16[4,64,2048]{2,1,0:T(8,128)(2,1)}), bf16[4,64,2048]{2,1,0:T(8,128)(2,1)S(1)}, u32[]{:S(2)}, u32[]{:S(2)}) %all-to-all-start.8) | async-done | bytes 1048608 | tf_op jit(solution)/shard_map/all_to_all | solution.py:19
  250.6 11.4 %shard_map.180 = (f32[256,1408]{1,0:T(8,128)}, f32[256,1408]{1,0:T(8,128)}, bf16[256,1408]{1,0:T(8,128)(2,1)}, bf16[256,2048]{1,0:T(8,128)(2,1)}) custom-call(s32[1,2]{1,0:T(1,128)} %iota.25.t, bf16[256,2048]{1,0:T(8,128)(2,1)} %bitcast.386, bf16[2,4,3,256,1408]{4,3,2,1,0:T(8,128)(2,1)} %bitcast.355), custom_call_target="tpu_custom_call" | custom-call | flops 4429185024 | bytes 17301504 | tf_op jit(solution)/shard_map/pallas_call | solution.py:63
  269.3 50.6 %all-to-all-done.10 = bf16[4,64,2048]{2,1,0:T(8,128)(2,1)S(1)} async-done(((bf16[4,64,2048]{2,1,0:T(8,128)(2,1)}), bf16[4,64,2048]{2,1,0:T(8,128)(2,1)S(1)}, u32[]{:S(2)}, u32[]{:S(2)}) %all-to-all-start.10) | async-done | bytes 1048608 | tf_op jit(solution)/shard_map/all_to_all | solution.py:19
  328.8 15.3 %all-gather.13.cloned.1.call-done = bf16[1,2048,2048]{2,1,0:T(8,128)(2,1)} async-done(((bf16[1,256,2048]{2,1,0:T(8,128)(2,1)}), bf16[1,2048,2048]{2,1,0:T(8,128)(2,1)}) %all-gather.13.cloned.1.call-update) | async-done | bytes 8388624 | tf_op jit(solution)/shard_map/all_gather | solution.py:561
  364.8 17.2 %all-to-all-done.12.o_ref = bf16[4,256,512]{2,1,0:T(8,128)(2,1)} async-done(((bf16[4,256,512]{2,1,0:T(8,128)(2,1)}), bf16[4,256,512]{2,1,0:T(8,128)(2,1)}, u32[]{:S(2)}, u32[]{:S(2)}) %all-to-all-start.12) | async-done | bytes 1048608 | tf_op jit(solution)/shard_map/all_to_all | solution.py:19
  413.4 17.5 %all-to-all-done.14 = bf16[4,64,2048]{2,1,0:T(8,128)(2,1)} async-done(((bf16[4,64,2048]{2,1,0:T(8,128)(2,1)}), bf16[4,64,2048]{2,1,0:T(8,128)(2,1)}, u32[]{:S(2)}, u32[]{:S(2)}) %all-to-all-start.14) | async-done | bytes 1048608 | tf_op jit(solution)/shard_map/all_to_all | solution.py:19
  430.9 11.4 %shard_map.183 = (f32[256,1408]{1,0:T(8,128)}, f32[256,1408]{1,0:T(8,128)}, bf16[256,1408]{1,0:T(8,128)(2,1)}, bf16[256,2048]{1,0:T(8,128)(2,1)}) custom-call(s32[1,2]{1,0:T(1,128)} %iota_xor_fusion.t, bf16[256,2048]{1,0:T(8,128)(2,1)} %bitcast.79.b_ref, bf16[2,4,2,256,1408]{4,3,2,1,0:T(8,128)(2,1)} %bitcast.357, bf16[4,256,1408]{2,1,0:T(8,128)(2,1)} %copy-done, ...), custom_call_target="tpu_custom_call" | custom-call | flops 4429185024 | bytes 17301504 | tf_op jit(solution)/shard_map/pallas_call | solution.py:63
  442.3 13.2 %shard_map.184 = (bf16[2,256,1408]{2,1,0:T(8,128)(2,1)}, bf16[256,2048]{1,0:T(8,128)(2,1)}) custom-call(s32[1,2]{1,0:T(1,128)} %iota_xor_fusion.t, bf16[256,2048]{1,0:T(8,128)(2,1)} %bitcast.76.dy_ref, f32[256,1408]{1,0:T(8,128)} %get-tuple-element.186.gate_ref, f32[256,1408]{1,0:T(8,128)} %get-tuple-element.187.up_ref, ...), custom_call_target="tpu_custom_call" | custom-call | flops 4429185024 | bytes 17301504 | tf_op jit(solution)/shard_map/pallas_call | solution.py:63
  465.7 10.1 %shard_map.185 = bf16[4,768,1408]{2,1,0:T(8,128)(2,1)} custom-call(s32[1,1]{1,0:T(1,128)} %bitcast.91._, bf16[256,2048]{1,0:T(8,128)(2,1)} %bitcast.79.b_ref, bf16[2,256,1408]{2,1,0:T(8,128)(2,1)} %get-tuple-element.193.d_ref, bf16[256,2048]{1,0:T(8,128)(2,1)} %bitcast.76.dy_ref, bf16[256,1408]{1,0:T(8,128)(2,1)} %get-tuple-element.195.m_ref, ...), custom_call_target="tpu_custom_call" | custom-call | flops 4429185024 | bytes 8650752 | tf_op jit(solution)/shard_map/pallas_call | solution.py:63
  475.7 10.1 %all-to-all-done.15 = bf16[4,64,2048]{2,1,0:T(8,128)(2,1)S(1)} async-done(((bf16[4,64,2048]{2,1,0:T(8,128)(2,1)}), bf16[4,64,2048]{2,1,0:T(8,128)(2,1)S(1)}, u32[]{:S(2)}, u32[]{:S(2)}) %all-to-all-start.15) | async-done | bytes 1048608 | tf_op jit(solution)/shard_map/all_to_all | solution.py:19
  487.5 12.2 %all_to_all.152 = bf16[4,64,512]{2,1,0:T(8,128)(2,1)} all-to-all(bf16[4,64,512]{2,1,0:T(8,128)(2,1)S(1)} %copy.129), channel_id=1, replica_groups=mesh['section'=2,'row'=4,'col'=4] {'col'}, dimensions={0} | all-to-all | bytes 524288 | tf_op jit(solution)/shard_map/all_to_all | solution.py:19
  514.5 18.5 %all-to-all-done.17 = bf16[4,256,512]{2,1,0:T(8,128)(2,1)S(1)} async-done(((bf16[4,256,512]{2,1,0:T(8,128)(2,1)}), bf16[4,256,512]{2,1,0:T(8,128)(2,1)S(1)}, u32[]{:S(2)}, u32[]{:S(2)}) %all-to-all-start.17) | async-done | bytes 1048608 | tf_op jit(solution)/shard_map/all_to_all | solution.py:19
  533.9 9.6 %shard_map.187 = (bf16[256,1536]{1,0:T(8,128)(2,1)}, f32[1,1536]{1,0:T(1,128)}, bf16[256,2048]{1,0:T(8,128)(2,1)}) custom-call(s32[1,1]{1,0:T(1,128)} %constant.233.clone.1._, bf16[256,512]{1,0:T(8,128)(2,1)} %reduce_sum.315.d_ref, bf16[256,1536]{1,0:T(8,128)(2,1)} %get-tuple-element.199.qkv_ref, bf16[2048,2048]{1,0:T(8,128)(2,1)} %bitcast.354, ...), custom_call_target="tpu_custom_call" | custom-call | flops 1610612736 | bytes 6291456 | tf_op jit(solution)/shard_map/pallas_call | solution.py:63
  548.4 16.0 %all-to-all-done.18 = bf16[4,64,2048]{2,1,0:T(8,128)(2,1)S(1)} async-done(((bf16[4,64,2048]{2,1,0:T(8,128)(2,1)}), bf16[4,64,2048]{2,1,0:T(8,128)(2,1)S(1)}, u32[]{:S(2)}, u32[]{:S(2)}) %all-to-all-start.18) | async-done | bytes 1048608 | tf_op jit(solution)/shard_map/all_to_all | solution.py:19
  574.3 28.7 %all_to_all.153 = bf16[4,64,2048]{2,1,0:T(8,128)(2,1)} all-to-all(bf16[4,64,2048]{2,1,0:T(8,128)(2,1)S(1)} %broadcast_in_dim.239), channel_id=1, replica_groups=mesh['section'=2,'row'=4,'col'=4] {'row'}, dimensions={0} | all-to-all | bytes 2097152 | tf_op jit(solution)/shard_map/all_to_all | solution.py:19
  603.5 13.9 %shard_map.189 = (bf16[2,256,1408]{2,1,0:T(8,128)(2,1)}, bf16[256,2048]{1,0:T(8,128)(2,1)}) custom-call(s32[1,2]{1,0:T(1,128)} %iota.28.t, bf16[256,2048]{1,0:T(8,128)(2,1)} %bitcast.383, f32[256,1408]{1,0:T(8,128)} %get-tuple-element.205.gate_ref, f32[256,1408]{1,0:T(8,128)} %get-tuple-element.206.up_ref, bf16[2,4,3,256,1408]{4,3,2,1,0:T(8,128)(2,1)} %bitcast.356), custom_call_target="tpu_custom_call" | custom-call | flops 4429185024 | bytes 17301504 | tf_op jit(solution)/shard_map/pallas_call | solution.py:63
  630.6 9.6 %shard_map.190 = (bf16[4,512,1408]{2,1,0:T(8,128)(2,1)}, bf16[4,256,1408]{2,1,0:T(8,128)(2,1)}) custom-call(s32[1,1]{1,0:T(1,128)} %bitcast.91._, bf16[256,2048]{1,0:T(8,128)(2,1)} %bitcast.388, bf16[2,256,1408]{2,1,0:T(8,128)(2,1)} %get-tuple-element.214.d_ref, bf16[256,2048]{1,0:T(8,128)(2,1)} %bitcast.384, bf16[256,1408]{1,0:T(8,128)(2,1)} %get-tuple-element.216.m_ref, ...), custom_call_target="tpu_custom_call" | custom-call | flops 4429185024 | bytes 8650752 | tf_op jit(solution)/shard_map/pallas_call | solution.py:63
  640.2 36.3 %all-to-all-done.20 = bf16[4,64,2048]{2,1,0:T(8,128)(2,1)S(1)} async-done(((bf16[4,64,2048]{2,1,0:T(8,128)(2,1)}), bf16[4,64,2048]{2,1,0:T(8,128)(2,1)S(1)}, u32[]{:S(2)}, u32[]{:S(2)}) %all-to-all-start.20) | async-done | bytes 1048608 | tf_op jit(solution)/shard_map/all_to_all | solution.py:19
  713.8 10.5 %all-to-all-done.22 = bf16[4,256,512]{2,1,0:T(8,128)(2,1)} async-done(((bf16[4,256,512]{2,1,0:T(8,128)(2,1)}), bf16[4,256,512]{2,1,0:T(8,128)(2,1)}, u32[]{:S(2)}, u32[]{:S(2)}) %all-to-all-start.22) | async-done | bytes 1048608 | tf_op jit(solution)/shard_map/all_to_all | solution.py:19
  726.5 11.2 %collective-permute-done.39 = bf16[128,1408]{1,0:T(8,128)(2,1)} collective-permute-done((bf16[128,1408]{1,0:T(8,128)(2,1)}, bf16[128,1408]{1,0:T(8,128)(2,1)}, u32[]{:S(2)}, u32[]{:S(2)}) %collective-permute-start.39) | collective-permute-done | bytes 360480 | tf_op jit(solution)/shard_map/ppermute | solution.py:479
  737.7 9.2 shard_map.192
  758.0 16.7 %all-to-all-done.23 = bf16[4,64,2048]{2,1,0:T(8,128)(2,1)} async-done(((bf16[4,64,2048]{2,1,0:T(8,128)(2,1)}), bf16[4,64,2048]{2,1,0:T(8,128)(2,1)}, u32[]{:S(2)}, u32[]{:S(2)}) %all-to-all-start.23) | async-done | bytes 1048608 | tf_op jit(solution)/shard_map/all_to_all | solution.py:19
  813.5 13.4 %collective-permute-done.46 = bf16[128,1408]{1,0:T(8,128)(2,1)} collective-permute-done((bf16[128,1408]{1,0:T(8,128)(2,1)S(1)}, bf16[128,1408]{1,0:T(8,128)(2,1)}, u32[]{:S(2)}, u32[]{:S(2)}) %collective-permute-start.46) | collective-permute-done | bytes 360480 | tf_op jit(solution)/shard_map/ppermute | solution.py:479
  847.8 11.0 %all-to-all-done.25 = bf16[4,128,1408]{2,1,0:T(8,128)(2,1)S(1)} async-done(((bf16[4,128,1408]{2,1,0:T(8,128)(2,1)}), bf16[4,128,1408]{2,1,0:T(8,128)(2,1)S(1)}, u32[]{:S(2)}, u32[]{:S(2)}) %all-to-all-start.25) | async-done | bytes 1441824 | tf_op jit(solution)/shard_map/all_to_all | solution.py:19
  876.7 8.9 collective-permute-done.60
  901.0 9.6 %copy.138 = f32[1,512,2,1408]{3,2,1,0:T(2,128)} copy(f32[1,512,2,1408]{3,1,2,0:T(8,128)} %convert_bitcast_fusion) | data formatting | bytes 11534336
  (547 shorter events, 427.5 us)
Async XLA Ops:
  7.2 138.0 %all-gather.11.cloned.1.call-start = ((), (), s32[]{:S(2)}) async-start(), calls=%async_computation.40 | async-start | bytes 9437184 | tf_op jit(solution)/shard_map/all_gather | solution.py:561
  39.2 40.0 %collective-permute-start.6 = (bf16[128,1408]{1,0:T(8,128)(2,1)}, bf16[128,1408]{1,0:T(8,128)(2,1)}, u32[]{:S(2)}, u32[]{:S(2)}) collective-permute-start(bf16[128,1408]{1,0:T(8,128)(2,1)} %get-tuple-element.390), channel_id=1, source_target_pairs={{0,1},{1,0},{2,3},{3,2},{4,5},{5,4},{6,7},{7,6},{8,9},{9,8},{10,11... | collective-permute-start | bytes 1081352 | tf_op jit(solution)/shard_map/ppermute | solution.py:479
  41.1 41.9 %collective-permute-start.7 = (bf16[128,1408]{1,0:T(8,128)(2,1)}, bf16[128,1408]{1,0:T(8,128)(2,1)}, u32[]{:S(2)}, u32[]{:S(2)}) collective-permute-start(bf16[128,1408]{1,0:T(8,128)(2,1)} %get-tuple-element.389), channel_id=1, source_target_pairs={{0,2},{1,3},{2,0},{3,1},{4,6},{5,7},{6,4},{7,5},{8,10},{9,11},{10,... | collective-permute-start | bytes 1081352 | tf_op jit(solution)/shard_map/ppermute | solution.py:479
  69.5 180.2 %all-gather.7.cloned.1.call-start = ((), (), s32[]{:S(2)}) async-start(), calls=%async_computation.34 | async-start | bytes 19464192 | tf_op jit(solution)/shard_map/all_gather | solution.py:574
  70.5 34.6 %collective-permute-start.3 = (bf16[128,1408]{1,0:T(8,128)(2,1)}, bf16[128,1408]{1,0:T(8,128)(2,1)S(1)}, u32[]{:S(2)}, u32[]{:S(2)}) collective-permute-start(bf16[128,1408]{1,0:T(8,128)(2,1)} %get-tuple-element.394), channel_id=1, source_target_pairs={{0,4},{4,0},{8,12},{12,8},{1,5},{5,1},{9,13},{13,9},{2,6},{6,2},{1... | collective-permute-start | bytes 1081352 | tf_op jit(solution)/shard_map/ppermute | solution.py:479
  71.9 38.2 %collective-permute-start.4 = (bf16[128,1408]{1,0:T(8,128)(2,1)}, bf16[128,1408]{1,0:T(8,128)(2,1)}, u32[]{:S(2)}, u32[]{:S(2)}) collective-permute-start(bf16[128,1408]{1,0:T(8,128)(2,1)} %get-tuple-element.393), channel_id=1, source_target_pairs={{0,8},{4,12},{8,0},{12,4},{1,9},{5,13},{9,1},{13,5},{2,10},{6,14},... | collective-permute-start | bytes 1081352 | tf_op jit(solution)/shard_map/ppermute | solution.py:479
  79.2 43.0 %collective-permute-start.5 = (bf16[128,1408]{1,0:T(8,128)(2,1)S(1)}, bf16[128,1408]{1,0:T(8,128)(2,1)S(1)}, u32[]{:S(2)}, u32[]{:S(2)}) collective-permute-start(bf16[128,1408]{1,0:T(8,128)(2,1)S(1)} %get-tuple-element.392), channel_id=1, source_target_pairs={{0,12},{4,8},{8,4},{12,0},{1,13},{5,9},{9,5},{13,1},{2,14},{6,10},... | collective-permute-start | bytes 1081352 | tf_op jit(solution)/shard_map/ppermute | solution.py:479
  159.2 184.8 %all-gather.13.cloned.1.call-start = ((), (), s32[]{:S(2)}) async-start(), calls=%async_computation.41 | async-start | bytes 9437184 | tf_op jit(solution)/shard_map/all_gather | solution.py:561
  161.4 41.1 %collective-permute-start.10 = (bf16[128,1408]{1,0:T(8,128)(2,1)}, bf16[128,1408]{1,0:T(8,128)(2,1)S(1)}, u32[]{:S(2)}, u32[]{:S(2)}) collective-permute-start(bf16[128,1408]{1,0:T(8,128)(2,1)} %get-tuple-element.385), channel_id=1, source_target_pairs={{0,8},{4,12},{8,0},{12,4},{1,9},{5,13},{9,1},{13,5},{2,10},{6,14},... | collective-permute-start | bytes 1081352 | tf_op jit(solution)/shard_map/ppermute | solution.py:479
  226.4 204.5 %all-gather.9.cloned.1.call-start = ((), (), s32[]{:S(2)}) async-start(), calls=%async_computation.35 | async-start | bytes 12976128 | tf_op jit(solution)/shard_map/all_gather | solution.py:574
  262.0 57.8 %all-to-all-start.10 = ((bf16[4,64,2048]{2,1,0:T(8,128)(2,1)}), bf16[4,64,2048]{2,1,0:T(8,128)(2,1)S(1)}, u32[]{:S(2)}, u32[]{:S(2)}) async-start(bf16[4,64,2048]{2,1,0:T(8,128)(2,1)} %bitcast.415), calls=%async_computation.10 | async-start | bytes 2097152 | tf_op jit(solution)/shard_map/all_to_all | solution.py:19
  265.7 54.3 %collective-permute-start.12 = (bf16[256,1408]{1,0:T(8,128)(2,1)S(1)}, bf16[256,1408]{1,0:T(8,128)(2,1)}, u32[]{:S(2)}, u32[]{:S(2)}) collective-permute-start(bf16[256,1408]{1,0:T(8,128)(2,1)S(1)} %copy-done.18), channel_id=1, source_target_pairs={{0,1},{1,0},{2,3},{3,2},{4,5},{5,4},{6,7},{7,6},{8,9},{9,8},{10,11... | collective-permute-start | bytes 2162696 | tf_op jit(solution)/shard_map/ppermute | solution.py:479
  267.1 52.9 %collective-permute-start.13 = (bf16[256,1408]{1,0:T(8,128)(2,1)S(1)}, bf16[256,1408]{1,0:T(8,128)(2,1)}, u32[]{:S(2)}, u32[]{:S(2)}) collective-permute-start(bf16[256,1408]{1,0:T(8,128)(2,1)S(1)} %copy-done.18), channel_id=1, source_target_pairs={{0,2},{1,3},{2,0},{3,1},{4,6},{5,7},{6,4},{7,5},{8,10},{9,11},{10,... | collective-permute-start | bytes 2162696 | tf_op jit(solution)/shard_map/ppermute | solution.py:479
  267.6 52.5 %collective-permute-start.14 = (bf16[256,1408]{1,0:T(8,128)(2,1)S(1)}, bf16[256,1408]{1,0:T(8,128)(2,1)S(1)}, u32[]{:S(2)}, u32[]{:S(2)}) collective-permute-start(bf16[256,1408]{1,0:T(8,128)(2,1)S(1)} %copy-done.18), channel_id=1, source_target_pairs={{0,3},{1,2},{2,1},{3,0},{4,7},{5,6},{6,5},{7,4},{8,11},{9,10},{10,... | collective-permute-start | bytes 2162696 | tf_op jit(solution)/shard_map/ppermute | solution.py:479
  459.2 158.3 %reduce-scatter.5.cloned.1.call-start = ((), (), s32[]{:S(2)}) async-start(), calls=%async_computation.36 | async-start | bytes 10813440 | tf_op jit(solution)/shard_map/reduce_scatter | solution.py:702
  514.0 50.7 %collective-permute-start.26 = (bf16[256,2048]{1,0:T(8,128)(2,1)}, bf16[256,2048]{1,0:T(8,128)(2,1)}, u32[]{:S(2)}, u32[]{:S(2)}) collective-permute-start(bf16[256,2048]{1,0:T(8,128)(2,1)} %bitcast.68.a_ref), channel_id=1, source_target_pairs={{0,16},{16,0},{1,17},{17,1},{2,18},{18,2},{3,19},{19,3},{4,20},{20... | collective-permute-start | bytes 3145736 | tf_op jit(solution)/shard_map/ppermute | solution.py:475
  514.0 50.7 %collective-permute-start.27 = (bf16[4,256,512]{2,1,0:T(8,128)(2,1)}, bf16[4,256,512]{2,1,0:T(8,128)(2,1)}, u32[]{:S(2)}, u32[]{:S(2)}) collective-permute-start(bf16[4,256,512]{2,1,0:T(8,128)(2,1)} %all-to-all-done.12.o_ref), channel_id=1, source_target_pairs={{0,16},{16,0},{1,17},{17,1},{2,18},{18,2},{3,19},{19,3},{4,20},{20... | collective-permute-start | bytes 3145736 | tf_op jit(solution)/shard_map/ppermute | solution.py:475
  547.2 179.3 %reduce-scatter.7.cloned.1.call-start = ((), (), s32[]{:S(2)}) async-start(), calls=%async_computation.37 | async-start | bytes 5242880 | tf_op jit(solution)/shard_map/reduce_scatter | solution.py:753
  620.0 56.4 %all-to-all-start.20 = ((bf16[4,64,2048]{2,1,0:T(8,128)(2,1)}), bf16[4,64,2048]{2,1,0:T(8,128)(2,1)S(1)}, u32[]{:S(2)}, u32[]{:S(2)}) async-start(bf16[4,64,2048]{2,1,0:T(8,128)(2,1)} %bitcast.412), calls=%async_computation.21 | async-start | bytes 2097152 | tf_op jit(solution)/shard_map/all_to_all | solution.py:19
  623.7 167.4 %reduce-scatter.9.cloned.1.call-start = ((), (), s32[]{:S(2)}) async-start(), calls=%async_computation.38 | async-start | bytes 7208960 | tf_op jit(solution)/shard_map/reduce_scatter | solution.py:702
  691.8 85.1 %collective-permute-start.41 = (bf16[256,2048]{1,0:T(8,128)(2,1)S(1)}, bf16[256,2048]{1,0:T(8,128)(2,1)}, u32[]{:S(2)}, u32[]{:S(2)}) collective-permute-start(bf16[256,2048]{1,0:T(8,128)(2,1)S(1)} %bitcast.367), channel_id=1, source_target_pairs={{0,16},{16,0},{1,17},{17,1},{2,18},{18,2},{3,19},{19,3},{4,20},{20... | collective-permute-start | bytes 3145736 | tf_op jit(solution)/shard_map/ppermute | solution.py:475
  691.8 86.6 %collective-permute-start.42 = (bf16[4,256,512]{2,1,0:T(8,128)(2,1)S(1)}, bf16[4,256,512]{2,1,0:T(8,128)(2,1)}, u32[]{:S(2)}, u32[]{:S(2)}) collective-permute-start(bf16[4,256,512]{2,1,0:T(8,128)(2,1)S(1)} %copy-done.4), channel_id=1, source_target_pairs={{0,16},{16,0},{1,17},{17,1},{2,18},{18,2},{3,19},{19,3},{4,20},{20... | collective-permute-start | bytes 3145736 | tf_op jit(solution)/shard_map/ppermute | solution.py:475
  726.5 53.4 %collective-permute-start.44 = (bf16[256,512]{1,0:T(8,128)(2,1)S(1)}, bf16[256,512]{1,0:T(8,128)(2,1)}, u32[]{:S(2)}, u32[]{:S(2)}) collective-permute-start(bf16[256,512]{1,0:T(8,128)(2,1)S(1)} %bitcast.397), channel_id=1, source_target_pairs={{0,16},{16,0},{1,17},{17,1},{2,18},{18,2},{3,19},{19,3},{4,20},{20... | collective-permute-start | bytes 786440 | tf_op jit(solution)/shard_map/ppermute | solution.py:475
  746.9 33.0 %collective-permute-start.43 = (bf16[256,1536]{1,0:T(8,128)(2,1)}, bf16[256,1536]{1,0:T(8,128)(2,1)}, u32[]{:S(2)}, u32[]{:S(2)}) collective-permute-start(bf16[256,1536]{1,0:T(8,128)(2,1)} %get-tuple-element.231.dp_ref), channel_id=1, source_target_pairs={{0,16},{16,0},{1,17},{17,1},{2,18},{18,2},{3,19},{19,3},{4,20},{20... | collective-permute-start | bytes 2359304 | tf_op jit(solution)/shard_map/ppermute | solution.py:475
  751.5 174.1 %reduce-scatter.11.cloned.1.call-start = ((), (), s32[]{:S(2)}) async-start(), calls=%async_computation.39 | async-start | bytes 5242880 | tf_op jit(solution)/shard_map/reduce_scatter | solution.py:753
  755.9 44.3 %collective-permute-start.48 = (bf16[128,1408]{1,0:T(8,128)(2,1)}, bf16[128,1408]{1,0:T(8,128)(2,1)}, u32[]{:S(2)}, u32[]{:S(2)}) collective-permute-start(bf16[128,1408]{1,0:T(8,128)(2,1)} %get-tuple-element.372), channel_id=1, source_target_pairs={{0,1},{1,0},{2,3},{3,2},{4,5},{5,4},{6,7},{7,6},{8,9},{9,8},{10,11... | collective-permute-start | bytes 1081352 | tf_op jit(solution)/shard_map/ppermute | solution.py:479
  777.0 32.0 %collective-permute-start.49 = (bf16[128,1408]{1,0:T(8,128)(2,1)}, bf16[128,1408]{1,0:T(8,128)(2,1)S(1)}, u32[]{:S(2)}, u32[]{:S(2)}) collective-permute-start(bf16[128,1408]{1,0:T(8,128)(2,1)} %get-tuple-element.371), channel_id=1, source_target_pairs={{0,2},{1,3},{2,0},{3,1},{4,6},{5,7},{6,4},{7,5},{8,10},{9,11},{10,... | collective-permute-start | bytes 1081352 | tf_op jit(solution)/shard_map/ppermute | solution.py:479
  844.9 31.8 %collective-permute-start.59 = (bf16[256,1408]{1,0:T(8,128)(2,1)}, bf16[256,1408]{1,0:T(8,128)(2,1)}, u32[]{:S(2)}, u32[]{:S(2)}) collective-permute-start(bf16[256,1408]{1,0:T(8,128)(2,1)} %get-tuple-element.362), channel_id=1, source_target_pairs={{0,2},{1,3},{2,0},{3,1},{4,6},{5,7},{6,4},{7,5},{8,10},{9,11},{10,... | collective-permute-start | bytes 2162696 | tf_op jit(solution)/shard_map/ppermute | solution.py:479
  846.4 39.3 %collective-permute-start.60 = (bf16[256,1408]{1,0:T(8,128)(2,1)}, bf16[256,1408]{1,0:T(8,128)(2,1)}, u32[]{:S(2)}, u32[]{:S(2)}) collective-permute-start(bf16[256,1408]{1,0:T(8,128)(2,1)} %get-tuple-element.361), channel_id=1, source_target_pairs={{0,3},{1,2},{2,1},{3,0},{4,7},{5,6},{6,5},{7,4},{8,11},{9,10},{10,... | collective-permute-start | bytes 2162696 | tf_op jit(solution)/shard_map/ppermute | solution.py:479
  859.4 51.4 %collective-permute-start.55 = (f32[2,7,512]{2,1,0:T(8,128)}, f32[2,7,512]{2,1,0:T(8,128)S(1)}, u32[]{:S(2)}, u32[]{:S(2)}) collective-permute-start(f32[2,7,512]{2,1,0:T(8,128)} %maximum_maximum_fusion), channel_id=1, source_target_pairs={{0,4},{4,0},{8,12},{12,8},{1,5},{5,1},{9,13},{13,9},{2,6},{6,2},{1... | collective-permute-start | bytes 86024 | tf_op jit(solution)/shard_map/ppermute | solution.py:479
  865.7 45.1 %collective-permute-start.56 = (f32[2,7,512]{2,1,0:T(8,128)}, f32[2,7,512]{2,1,0:T(8,128)S(1)}, u32[]{:S(2)}, u32[]{:S(2)}) collective-permute-start(f32[2,7,512]{2,1,0:T(8,128)} %maximum_maximum_fusion), channel_id=1, source_target_pairs={{0,8},{4,12},{8,0},{12,4},{1,9},{5,13},{9,1},{13,5},{2,10},{6,14},... | collective-permute-start | bytes 86024 | tf_op jit(solution)/shard_map/ppermute | solution.py:479
  874.3 36.4 %collective-permute-start.57 = (f32[2,7,512]{2,1,0:T(8,128)}, f32[2,7,512]{2,1,0:T(8,128)S(1)}, u32[]{:S(2)}, u32[]{:S(2)}) collective-permute-start(f32[2,7,512]{2,1,0:T(8,128)} %maximum_maximum_fusion), channel_id=1, source_target_pairs={{0,12},{4,8},{8,4},{12,0},{1,13},{5,9},{9,5},{13,1},{2,14},{6,10},... | collective-permute-start | bytes 86024 | tf_op jit(solution)/shard_map/ppermute | solution.py:479
  (141 other events, 1796.0 us)
Sparse Core Ops, SparseCore 0:
  17.0 113.3 all-gather.10
  132.8 105.2 all-gather.6
  239.7 104.2 all-gather.12
  345.8 80.1 all-gather.8
  486.1 110.5 reduce-scatter.4
  598.9 93.5 reduce-scatter.6
  696.3 94.7 reduce-scatter.8
  833.3 82.6 reduce-scatter.10

commit v2 on v1

--- a/solution.py
+++ b/solution.py
@@ -468,6 +468,28 @@
         dy,
         m,
         *mates,
+    )
+
+
+def interleave(x):
+    _, n, f = x.shape
+    rows = 64 if n % 64 == 0 else n
+
+    def body(_, x_ref, out_ref):
+        for i in range(2):
+            out_ref[:, i, :] = x_ref[i].astype(F32)
+
+    return call(
+        body,
+        n // rows,
+        [pl.BlockSpec((2, rows, f), lambda i, t: (0, i, 0))],
+        pl.BlockSpec((rows, 2, f), lambda i, t: (i, 0, 0)),
+        jax.ShapeDtypeStruct((n, 2, f), F32),
+        [],
+        2 * n * f,
+        12 * n * f,
+        no_table(),
+        x,
     )
 
 
@@ -761,7 +783,7 @@
         jnp.stack(qo_grads[:3], axis=1)[None],
         sums[None, 4:],
         qo_grads[3][None],
-        g_grads.astype(F32).transpose(1, 0, 2)[None],
+        interleave(g_grads)[None],
         unshare(d_grads).astype(F32).reshape(dc, fr).T[None],
         sums[None, 0:2],
         sums[None, 2:4],

time: 962 us -> 953 us (level)
  local copies, waits for them, and re-layouts: 112 us -> 101 us
    unnamed x173 -> x194, local copies, waits for them, and re-layouts: 28.6 us -> 20.6 us
    pallas_call x16 -> x17, Pallas kernels: 137 us -> 143 us  [call(): pl.pallas_call(body, grid_spec=pltpu.PrefetchScalarGridSpec(num_scalar_pr...]
  transfers between devices with their start and end apart: 91 -> 91, of which waited for: 37 -> 36; matrix products, arithmetic and copies ran while one was open for 12% -> 11% of each run, Pallas kernels for 12% -> 13%
where the time goes in v2:
time: 953 us; the launch traced here: 935 us
  waiting for transfers between devices  376 us (39%)
  starting transfers between devices  187 us (20%)
  Pallas kernels  143 us (15%)
  local copies, waits for them, and re-layouts  101 us (11%)
  blocking collectives  79.4 us (8%)
  other arithmetic  32.5 us (3%)
  between operations  16.4 us (2%)
    all_to_all x22, waiting for transfers between devices, trade(): return lax.all_to_all(stack, axis, split_axis=0, concat_axis=0)  250 us
    pallas_call x17, Pallas kernels, call(): pl.pallas_call(body, grid_spec=pltpu.PrefetchScalarGridSpec(num_scalar_pr...  143 us
    ppermute x42, waiting for transfers between devices, hop(): lax.ppermute(value, axis, [(i, i ^ step) for i in range(lax.axis_size(axi...  99.6 us
    ppermute x42, starting transfers between devices, hop(): lax.ppermute(value, axis, [(i, i ^ step) for i in range(lax.axis_size(axi...  94.8 us
    all_to_all x22, starting transfers between devices, trade(): return lax.all_to_all(stack, axis, split_axis=0, concat_axis=0)  87 us
    all_to_all x8, blocking collectives, trade(): return lax.all_to_all(stack, axis, split_axis=0, concat_axis=0)  79.4 us
    dynamic_update_slice x36, local copies, waits for them, and re-layouts, place_all(): out = lax.dynamic_update_index_in_dim(out, piece, me ^ k, 0)  26.2 us
    unnamed x194, local copies, waits for them, and re-layouts  20.6 us
  transfers between devices with their start and end apart: 91, of which 36 were waited for; matrix products, arithmetic and copies ran while one was open for 11% of the time, Pallas kernels for 13%

profile of v2, /device:TPU:0, one launch (start us, length us, event | category | flops | bytes accessed | tf_op | source)
XLA Modules:
  0.0 935.2 jit_solution(16189875216909130847)
XLA Ops:
  81.9 22.2 %collective-permute-done.3 = bf16[128,1408]{1,0:T(8,128)(2,1)S(1)} collective-permute-done((bf16[128,1408]{1,0:T(8,128)(2,1)}, bf16[128,1408]{1,0:T(8,128)(2,1)S(1)}, u32[]{:S(2)}, u32[]{:S(2)}) %collective-permute-start.3) | collective-permute-done | bytes 360480 | tf_op jit(solution)/shard_map/ppermute | solution.py:501
  109.3 11.8 %collective-permute-done.5 = bf16[128,1408]{1,0:T(8,128)(2,1)S(1)} collective-permute-done((bf16[128,1408]{1,0:T(8,128)(2,1)S(1)}, bf16[128,1408]{1,0:T(8,128)(2,1)S(1)}, u32[]{:S(2)}, u32[]{:S(2)}) %collective-permute-start.5) | collective-permute-done | bytes 360480 | tf_op jit(solution)/shard_map/ppermute | solution.py:501
  133.3 9.2 all-to-all-done.5
  158.8 18.7 %collective-permute-start.10 = (bf16[128,1408]{1,0:T(8,128)(2,1)}, bf16[128,1408]{1,0:T(8,128)(2,1)S(1)}, u32[]{:S(2)}, u32[]{:S(2)}) collective-permute-start(bf16[128,1408]{1,0:T(8,128)(2,1)} %get-tuple-element.349), channel_id=1, source_target_pairs={{0,8},{4,12},{8,0},{12,4},{1,9},{5,13},{9,1},{13,5},{2,10},{6,14},... | collective-permute-start | bytes 1081352 | tf_op jit(solution)/shard_map/ppermute | solution.py:501
  188.7 13.3 %collective-permute-done.10 = bf16[128,1408]{1,0:T(8,128)(2,1)S(1)} collective-permute-done((bf16[128,1408]{1,0:T(8,128)(2,1)}, bf16[128,1408]{1,0:T(8,128)(2,1)S(1)}, u32[]{:S(2)}, u32[]{:S(2)}) %collective-permute-start.10) | collective-permute-done | bytes 360480 | tf_op jit(solution)/shard_map/ppermute | solution.py:501
  202.1 12.0 %all_to_all.151 = bf16[4,64,512]{2,1,0:T(8,128)(2,1)S(1)} all-to-all(bf16[4,64,512]{2,1,0:T(8,128)(2,1)} %bitcast.409), channel_id=1, replica_groups=mesh['section'=2,'row'=4,'col'=4] {'col'}, dimensions={0} | all-to-all | bytes 524288 | tf_op jit(solution)/shard_map/all_to_all | solution.py:19
  226.6 21.7 %all-to-all-done.8 = bf16[4,64,2048]{2,1,0:T(8,128)(2,1)S(1)} async-done(((bf16[4,64,2048]{2,1,0:T(8,128)(2,1)}), bf16[4,64,2048]{2,1,0:T(8,128)(2,1)S(1)}, u32[]{:S(2)}, u32[]{:S(2)}) %all-to-all-start.8) | async-done | bytes 1048608 | tf_op jit(solution)/shard_map/all_to_all | solution.py:19
  249.3 11.4 %shard_map.180 = (f32[256,1408]{1,0:T(8,128)}, f32[256,1408]{1,0:T(8,128)}, bf16[256,1408]{1,0:T(8,128)(2,1)}, bf16[256,2048]{1,0:T(8,128)(2,1)}) custom-call(s32[1,2]{1,0:T(1,128)} %iota.25.t, bf16[256,2048]{1,0:T(8,128)(2,1)} %bitcast.384, bf16[2,4,3,256,1408]{4,3,2,1,0:T(8,128)(2,1)} %bitcast.352), custom_call_target="tpu_custom_call" | custom-call | flops 4429185024 | bytes 17301504 | tf_op jit(solution)/shard_map/pallas_call | solution.py:63
  268.0 50.8 %all-to-all-done.10 = bf16[4,64,2048]{2,1,0:T(8,128)(2,1)S(1)} async-done(((bf16[4,64,2048]{2,1,0:T(8,128)(2,1)}), bf16[4,64,2048]{2,1,0:T(8,128)(2,1)S(1)}, u32[]{:S(2)}, u32[]{:S(2)}) %all-to-all-start.10) | async-done | bytes 1048608 | tf_op jit(solution)/shard_map/all_to_all | solution.py:19
  327.8 16.2 %all-gather.13.cloned.1.call-done = bf16[1,2048,2048]{2,1,0:T(8,128)(2,1)} async-done(((bf16[1,256,2048]{2,1,0:T(8,128)(2,1)}), bf16[1,2048,2048]{2,1,0:T(8,128)(2,1)}) %all-gather.13.cloned.1.call-update) | async-done | bytes 8388624 | tf_op jit(solution)/shard_map/all_gather | solution.py:583
  364.7 17.2 %all-to-all-done.12.o_ref = bf16[4,256,512]{2,1,0:T(8,128)(2,1)} async-done(((bf16[4,256,512]{2,1,0:T(8,128)(2,1)}), bf16[4,256,512]{2,1,0:T(8,128)(2,1)}, u32[]{:S(2)}, u32[]{:S(2)}) %all-to-all-start.12) | async-done | bytes 1048608 | tf_op jit(solution)/shard_map/all_to_all | solution.py:19
  391.2 7.6 all-to-all-done.13
  413.3 17.6 %all-to-all-done.14 = bf16[4,64,2048]{2,1,0:T(8,128)(2,1)} async-done(((bf16[4,64,2048]{2,1,0:T(8,128)(2,1)}), bf16[4,64,2048]{2,1,0:T(8,128)(2,1)}, u32[]{:S(2)}, u32[]{:S(2)}) %all-to-all-start.14) | async-done | bytes 1048608 | tf_op jit(solution)/shard_map/all_to_all | solution.py:19
  430.9 11.4 %shard_map.183 = (f32[256,1408]{1,0:T(8,128)}, f32[256,1408]{1,0:T(8,128)}, bf16[256,1408]{1,0:T(8,128)(2,1)}, bf16[256,2048]{1,0:T(8,128)(2,1)}) custom-call(s32[1,2]{1,0:T(1,128)} %iota_xor_fusion.t, bf16[256,2048]{1,0:T(8,128)(2,1)} %bitcast.79.b_ref, bf16[2,4,2,256,1408]{4,3,2,1,0:T(8,128)(2,1)} %bitcast.354, bf16[4,256,1408]{2,1,0:T(8,128)(2,1)} %copy-done, ...), custom_call_target="tpu_custom_call" | custom-call | flops 4429185024 | bytes 17301504 | tf_op jit(solution)/shard_map/pallas_call | solution.py:63
  442.3 13.2 %shard_map.184 = (bf16[2,256,1408]{2,1,0:T(8,128)(2,1)}, bf16[256,2048]{1,0:T(8,128)(2,1)}) custom-call(s32[1,2]{1,0:T(1,128)} %iota_xor_fusion.t, bf16[256,2048]{1,0:T(8,128)(2,1)} %bitcast.76.dy_ref, f32[256,1408]{1,0:T(8,128)} %get-tuple-element.186.gate_ref, f32[256,1408]{1,0:T(8,128)} %get-tuple-element.187.up_ref, ...), custom_call_target="tpu_custom_call" | custom-call | flops 4429185024 | bytes 17301504 | tf_op jit(solution)/shard_map/pallas_call | solution.py:63
  466.6 10.0 %shard_map.185 = bf16[4,768,1408]{2,1,0:T(8,128)(2,1)} custom-call(s32[1,1]{1,0:T(1,128)} %bitcast.91._, bf16[256,2048]{1,0:T(8,128)(2,1)} %bitcast.79.b_ref, bf16[2,256,1408]{2,1,0:T(8,128)(2,1)} %get-tuple-element.193.d_ref, bf16[256,2048]{1,0:T(8,128)(2,1)} %bitcast.76.dy_ref, bf16[256,1408]{1,0:T(8,128)(2,1)} %get-tuple-element.195.m_ref, ...), custom_call_target="tpu_custom_call" | custom-call | flops 4429185024 | bytes 8650752 | tf_op jit(solution)/shard_map/pallas_call | solution.py:63
  476.6 9.2 all-to-all-done.15
  488.1 11.8 %all_to_all.152 = bf16[4,64,512]{2,1,0:T(8,128)(2,1)} all-to-all(bf16[4,64,512]{2,1,0:T(8,128)(2,1)S(1)} %copy.123), channel_id=1, replica_groups=mesh['section'=2,'row'=4,'col'=4] {'col'}, dimensions={0} | all-to-all | bytes 524288 | tf_op jit(solution)/shard_map/all_to_all | solution.py:19
  514.6 18.5 %all-to-all-done.17 = bf16[4,256,512]{2,1,0:T(8,128)(2,1)S(1)} async-done(((bf16[4,256,512]{2,1,0:T(8,128)(2,1)}), bf16[4,256,512]{2,1,0:T(8,128)(2,1)S(1)}, u32[]{:S(2)}, u32[]{:S(2)}) %all-to-all-start.17) | async-done | bytes 1048608 | tf_op jit(solution)/shard_map/all_to_all | solution.py:19
  534.7 9.2 shard_map.187
  548.8 15.7 %all-to-all-done.18 = bf16[4,64,2048]{2,1,0:T(8,128)(2,1)S(1)} async-done(((bf16[4,64,2048]{2,1,0:T(8,128)(2,1)}), bf16[4,64,2048]{2,1,0:T(8,128)(2,1)S(1)}, u32[]{:S(2)}, u32[]{:S(2)}) %all-to-all-start.18) | async-done | bytes 1048608 | tf_op jit(solution)/shard_map/all_to_all | solution.py:19
  574.3 28.7 %all_to_all.153 = bf16[4,64,2048]{2,1,0:T(8,128)(2,1)} all-to-all(bf16[4,64,2048]{2,1,0:T(8,128)(2,1)S(1)} %broadcast_in_dim.236), channel_id=1, replica_groups=mesh['section'=2,'row'=4,'col'=4] {'row'}, dimensions={0} | all-to-all | bytes 2097152 | tf_op jit(solution)/shard_map/all_to_all | solution.py:19
  603.5 13.9 %shard_map.189 = (bf16[2,256,1408]{2,1,0:T(8,128)(2,1)}, bf16[256,2048]{1,0:T(8,128)(2,1)}) custom-call(s32[1,2]{1,0:T(1,128)} %iota.28.t, bf16[256,2048]{1,0:T(8,128)(2,1)} %bitcast.381, f32[256,1408]{1,0:T(8,128)} %get-tuple-element.205.gate_ref, f32[256,1408]{1,0:T(8,128)} %get-tuple-element.206.up_ref, bf16[2,4,3,256,1408]{4,3,2,1,0:T(8,128)(2,1)} %bitcast.353), custom_call_target="tpu_custom_call" | custom-call | flops 4429185024 | bytes 17301504 | tf_op jit(solution)/shard_map/pallas_call | solution.py:63
  630.6 9.6 %shard_map.190 = (bf16[4,512,1408]{2,1,0:T(8,128)(2,1)}, bf16[4,256,1408]{2,1,0:T(8,128)(2,1)}) custom-call(s32[1,1]{1,0:T(1,128)} %bitcast.91._, bf16[256,2048]{1,0:T(8,128)(2,1)} %bitcast.386, bf16[2,256,1408]{2,1,0:T(8,128)(2,1)} %get-tuple-element.214.d_ref, bf16[256,2048]{1,0:T(8,128)(2,1)} %bitcast.382, bf16[256,1408]{1,0:T(8,128)(2,1)} %get-tuple-element.216.m_ref, ...), custom_call_target="tpu_custom_call" | custom-call | flops 4429185024 | bytes 8650752 | tf_op jit(solution)/shard_map/pallas_call | solution.py:63
  640.2 36.3 %all-to-all-done.20 = bf16[4,64,2048]{2,1,0:T(8,128)(2,1)S(1)} async-done(((bf16[4,64,2048]{2,1,0:T(8,128)(2,1)}), bf16[4,64,2048]{2,1,0:T(8,128)(2,1)S(1)}, u32[]{:S(2)}, u32[]{:S(2)}) %all-to-all-start.20) | async-done | bytes 1048608 | tf_op jit(solution)/shard_map/all_to_all | solution.py:19
  714.0 8.9 all-to-all-done.22
  723.9 14.1 %collective-permute-done.39 = bf16[128,1408]{1,0:T(8,128)(2,1)} collective-permute-done((bf16[128,1408]{1,0:T(8,128)(2,1)}, bf16[128,1408]{1,0:T(8,128)(2,1)}, u32[]{:S(2)}, u32[]{:S(2)}) %collective-permute-start.39) | collective-permute-done | bytes 360480 | tf_op jit(solution)/shard_map/ppermute | solution.py:501
  738.0 9.2 shard_map.192
  758.6 18.0 %all-to-all-done.23 = bf16[4,64,2048]{2,1,0:T(8,128)(2,1)} async-done(((bf16[4,64,2048]{2,1,0:T(8,128)(2,1)}), bf16[4,64,2048]{2,1,0:T(8,128)(2,1)}, u32[]{:S(2)}, u32[]{:S(2)}) %all-to-all-start.23) | async-done | bytes 1048608 | tf_op jit(solution)/shard_map/all_to_all | solution.py:19
  812.9 14.0 %collective-permute-done.46 = bf16[128,1408]{1,0:T(8,128)(2,1)S(1)} collective-permute-done((bf16[128,1408]{1,0:T(8,128)(2,1)S(1)}, bf16[128,1408]{1,0:T(8,128)(2,1)S(1)}, u32[]{:S(2)}, u32[]{:S(2)}) %collective-permute-start.46) | collective-permute-done | bytes 360480 | tf_op jit(solution)/shard_map/ppermute | solution.py:501
  846.8 9.9 %all-to-all-done.25 = bf16[4,128,1408]{2,1,0:T(8,128)(2,1)S(1)} async-done(((bf16[4,128,1408]{2,1,0:T(8,128)(2,1)}), bf16[4,128,1408]{2,1,0:T(8,128)(2,1)S(1)}, u32[]{:S(2)}, u32[]{:S(2)}) %all-to-all-start.25) | async-done | bytes 1441824 | tf_op jit(solution)/shard_map/all_to_all | solution.py:19
  874.7 8.0 collective-permute-done.60
  (568 shorter events, 419.0 us)
Async XLA Ops:
  7.2 135.3 %all-gather.11.cloned.1.call-start = ((), (), s32[]{:S(2)}) async-start(), calls=%async_computation.40 | async-start | bytes 9437184 | tf_op jit(solution)/shard_map/all_gather | solution.py:583
  39.3 38.7 %collective-permute-start.6 = (bf16[128,1408]{1,0:T(8,128)(2,1)}, bf16[128,1408]{1,0:T(8,128)(2,1)}, u32[]{:S(2)}, u32[]{:S(2)}) collective-permute-start(bf16[128,1408]{1,0:T(8,128)(2,1)} %get-tuple-element.354), channel_id=1, source_target_pairs={{0,1},{1,0},{2,3},{3,2},{4,5},{5,4},{6,7},{7,6},{8,9},{9,8},{10,11... | collective-permute-start | bytes 1081352 | tf_op jit(solution)/shard_map/ppermute | solution.py:501
  41.3 40.6 %collective-permute-start.7 = (bf16[128,1408]{1,0:T(8,128)(2,1)}, bf16[128,1408]{1,0:T(8,128)(2,1)}, u32[]{:S(2)}, u32[]{:S(2)}) collective-permute-start(bf16[128,1408]{1,0:T(8,128)(2,1)} %get-tuple-element.353), channel_id=1, source_target_pairs={{0,2},{1,3},{2,0},{3,1},{4,6},{5,7},{6,4},{7,5},{8,10},{9,11},{10,... | collective-permute-start | bytes 1081352 | tf_op jit(solution)/shard_map/ppermute | solution.py:501
  68.4 180.0 %all-gather.7.cloned.1.call-start = ((), (), s32[]{:S(2)}) async-start(), calls=%async_computation.34 | async-start | bytes 19464192 | tf_op jit(solution)/shard_map/all_gather | solution.py:596
  69.4 34.7 %collective-permute-start.3 = (bf16[128,1408]{1,0:T(8,128)(2,1)}, bf16[128,1408]{1,0:T(8,128)(2,1)S(1)}, u32[]{:S(2)}, u32[]{:S(2)}) collective-permute-start(bf16[128,1408]{1,0:T(8,128)(2,1)} %get-tuple-element.358), channel_id=1, source_target_pairs={{0,4},{4,0},{8,12},{12,8},{1,5},{5,1},{9,13},{13,9},{2,6},{6,2},{1... | collective-permute-start | bytes 1081352 | tf_op jit(solution)/shard_map/ppermute | solution.py:501
  71.0 38.3 %collective-permute-start.4 = (bf16[128,1408]{1,0:T(8,128)(2,1)}, bf16[128,1408]{1,0:T(8,128)(2,1)}, u32[]{:S(2)}, u32[]{:S(2)}) collective-permute-start(bf16[128,1408]{1,0:T(8,128)(2,1)} %get-tuple-element.357), channel_id=1, source_target_pairs={{0,8},{4,12},{8,0},{12,4},{1,9},{5,13},{9,1},{13,5},{2,10},{6,14},... | collective-permute-start | bytes 1081352 | tf_op jit(solution)/shard_map/ppermute | solution.py:501
  78.0 43.0 %collective-permute-start.5 = (bf16[128,1408]{1,0:T(8,128)(2,1)S(1)}, bf16[128,1408]{1,0:T(8,128)(2,1)S(1)}, u32[]{:S(2)}, u32[]{:S(2)}) collective-permute-start(bf16[128,1408]{1,0:T(8,128)(2,1)S(1)} %get-tuple-element.356), channel_id=1, source_target_pairs={{0,12},{4,8},{8,4},{12,0},{1,13},{5,9},{9,5},{13,1},{2,14},{6,10},... | collective-permute-start | bytes 1081352 | tf_op jit(solution)/shard_map/ppermute | solution.py:501
  156.6 187.4 %all-gather.13.cloned.1.call-start = ((), (), s32[]{:S(2)}) async-start(), calls=%async_computation.41 | async-start | bytes 9437184 | tf_op jit(solution)/shard_map/all_gather | solution.py:583
  158.8 43.2 %collective-permute-start.10 = (bf16[128,1408]{1,0:T(8,128)(2,1)}, bf16[128,1408]{1,0:T(8,128)(2,1)S(1)}, u32[]{:S(2)}, u32[]{:S(2)}) collective-permute-start(bf16[128,1408]{1,0:T(8,128)(2,1)} %get-tuple-element.349), channel_id=1, source_target_pairs={{0,8},{4,12},{8,0},{12,4},{1,9},{5,13},{9,1},{13,5},{2,10},{6,14},... | collective-permute-start | bytes 1081352 | tf_op jit(solution)/shard_map/ppermute | solution.py:501
  225.4 205.5 %all-gather.9.cloned.1.call-start = ((), (), s32[]{:S(2)}) async-start(), calls=%async_computation.35 | async-start | bytes 12976128 | tf_op jit(solution)/shard_map/all_gather | solution.py:596
  260.7 58.1 %all-to-all-start.10 = ((bf16[4,64,2048]{2,1,0:T(8,128)(2,1)}), bf16[4,64,2048]{2,1,0:T(8,128)(2,1)S(1)}, u32[]{:S(2)}, u32[]{:S(2)}) async-start(bf16[4,64,2048]{2,1,0:T(8,128)(2,1)} %bitcast.413), calls=%async_computation.10 | async-start | bytes 2097152 | tf_op jit(solution)/shard_map/all_to_all | solution.py:19
  264.4 54.6 %collective-permute-start.12 = (bf16[256,1408]{1,0:T(8,128)(2,1)S(1)}, bf16[256,1408]{1,0:T(8,128)(2,1)}, u32[]{:S(2)}, u32[]{:S(2)}) collective-permute-start(bf16[256,1408]{1,0:T(8,128)(2,1)S(1)} %copy-done.18), channel_id=1, source_target_pairs={{0,1},{1,0},{2,3},{3,2},{4,5},{5,4},{6,7},{7,6},{8,9},{9,8},{10,11... | collective-permute-start | bytes 2162696 | tf_op jit(solution)/shard_map/ppermute | solution.py:501
  265.9 53.1 %collective-permute-start.13 = (bf16[256,1408]{1,0:T(8,128)(2,1)S(1)}, bf16[256,1408]{1,0:T(8,128)(2,1)}, u32[]{:S(2)}, u32[]{:S(2)}) collective-permute-start(bf16[256,1408]{1,0:T(8,128)(2,1)S(1)} %copy-done.18), channel_id=1, source_target_pairs={{0,2},{1,3},{2,0},{3,1},{4,6},{5,7},{6,4},{7,5},{8,10},{9,11},{10,... | collective-permute-start | bytes 2162696 | tf_op jit(solution)/shard_map/ppermute | solution.py:501
  266.6 52.5 %collective-permute-start.14 = (bf16[256,1408]{1,0:T(8,128)(2,1)S(1)}, bf16[256,1408]{1,0:T(8,128)(2,1)S(1)}, u32[]{:S(2)}, u32[]{:S(2)}) collective-permute-start(bf16[256,1408]{1,0:T(8,128)(2,1)S(1)} %copy-done.18), channel_id=1, source_target_pairs={{0,3},{1,2},{2,1},{3,0},{4,7},{5,6},{6,5},{7,4},{8,11},{9,10},{10,... | collective-permute-start | bytes 2162696 | tf_op jit(solution)/shard_map/ppermute | solution.py:501
  459.2 158.4 %reduce-scatter.5.cloned.1.call-start = ((), (), s32[]{:S(2)}) async-start(), calls=%async_computation.36 | async-start | bytes 10813440 | tf_op jit(solution)/shard_map/reduce_scatter | solution.py:724
  514.1 50.6 %collective-permute-start.26 = (bf16[256,2048]{1,0:T(8,128)(2,1)}, bf16[256,2048]{1,0:T(8,128)(2,1)}, u32[]{:S(2)}, u32[]{:S(2)}) collective-permute-start(bf16[256,2048]{1,0:T(8,128)(2,1)} %bitcast.68.a_ref), channel_id=1, source_target_pairs={{0,16},{16,0},{1,17},{17,1},{2,18},{18,2},{3,19},{19,3},{4,20},{20... | collective-permute-start | bytes 3145736 | tf_op jit(solution)/shard_map/ppermute | solution.py:497
  514.1 50.6 %collective-permute-start.27 = (bf16[4,256,512]{2,1,0:T(8,128)(2,1)}, bf16[4,256,512]{2,1,0:T(8,128)(2,1)}, u32[]{:S(2)}, u32[]{:S(2)}) collective-permute-start(bf16[4,256,512]{2,1,0:T(8,128)(2,1)} %all-to-all-done.12.o_ref), channel_id=1, source_target_pairs={{0,16},{16,0},{1,17},{17,1},{2,18},{18,2},{3,19},{19,3},{4,20},{20... | collective-permute-start | bytes 3145736 | tf_op jit(solution)/shard_map/ppermute | solution.py:497
  547.6 176.3 %reduce-scatter.7.cloned.1.call-start = ((), (), s32[]{:S(2)}) async-start(), calls=%async_computation.37 | async-start | bytes 5242880 | tf_op jit(solution)/shard_map/reduce_scatter | solution.py:775
  620.1 56.5 %all-to-all-start.20 = ((bf16[4,64,2048]{2,1,0:T(8,128)(2,1)}), bf16[4,64,2048]{2,1,0:T(8,128)(2,1)S(1)}, u32[]{:S(2)}, u32[]{:S(2)}) async-start(bf16[4,64,2048]{2,1,0:T(8,128)(2,1)} %bitcast.410), calls=%async_computation.21 | async-start | bytes 2097152 | tf_op jit(solution)/shard_map/all_to_all | solution.py:19
  623.8 166.9 %reduce-scatter.9.cloned.1.call-start = ((), (), s32[]{:S(2)}) async-start(), calls=%async_computation.38 | async-start | bytes 7208960 | tf_op jit(solution)/shard_map/reduce_scatter | solution.py:724
  691.4 86.6 %collective-permute-start.41 = (bf16[256,2048]{1,0:T(8,128)(2,1)S(1)}, bf16[256,2048]{1,0:T(8,128)(2,1)}, u32[]{:S(2)}, u32[]{:S(2)}) collective-permute-start(bf16[256,2048]{1,0:T(8,128)(2,1)S(1)} %bitcast.364), channel_id=1, source_target_pairs={{0,16},{16,0},{1,17},{17,1},{2,18},{18,2},{3,19},{19,3},{4,20},{20... | collective-permute-start | bytes 3145736 | tf_op jit(solution)/shard_map/ppermute | solution.py:497
  691.4 88.0 %collective-permute-start.42 = (bf16[4,256,512]{2,1,0:T(8,128)(2,1)S(1)}, bf16[4,256,512]{2,1,0:T(8,128)(2,1)}, u32[]{:S(2)}, u32[]{:S(2)}) collective-permute-start(bf16[4,256,512]{2,1,0:T(8,128)(2,1)S(1)} %copy-done.5), channel_id=1, source_target_pairs={{0,16},{16,0},{1,17},{17,1},{2,18},{18,2},{3,19},{19,3},{4,20},{20... | collective-permute-start | bytes 3145736 | tf_op jit(solution)/shard_map/ppermute | solution.py:497
  706.8 31.1 %collective-permute-start.39 = (bf16[128,1408]{1,0:T(8,128)(2,1)}, bf16[128,1408]{1,0:T(8,128)(2,1)}, u32[]{:S(2)}, u32[]{:S(2)}) collective-permute-start(bf16[128,1408]{1,0:T(8,128)(2,1)} %get-tuple-element.343), channel_id=1, source_target_pairs={{0,8},{4,12},{8,0},{12,4},{1,9},{5,13},{9,1},{13,5},{2,10},{6,14},... | collective-permute-start | bytes 1081352 | tf_op jit(solution)/shard_map/ppermute | solution.py:501
  723.9 57.2 %collective-permute-start.44 = (bf16[256,512]{1,0:T(8,128)(2,1)}, bf16[256,512]{1,0:T(8,128)(2,1)S(1)}, u32[]{:S(2)}, u32[]{:S(2)}) collective-permute-start(bf16[256,512]{1,0:T(8,128)(2,1)} %bitcast.394), channel_id=1, source_target_pairs={{0,16},{16,0},{1,17},{17,1},{2,18},{18,2},{3,19},{19,3},{4,20},{20... | collective-permute-start | bytes 786440 | tf_op jit(solution)/shard_map/ppermute | solution.py:497
  747.2 33.8 %collective-permute-start.43 = (bf16[256,1536]{1,0:T(8,128)(2,1)}, bf16[256,1536]{1,0:T(8,128)(2,1)}, u32[]{:S(2)}, u32[]{:S(2)}) collective-permute-start(bf16[256,1536]{1,0:T(8,128)(2,1)} %get-tuple-element.231.dp_ref), channel_id=1, source_target_pairs={{0,16},{16,0},{1,17},{17,1},{2,18},{18,2},{3,19},{19,3},{4,20},{20... | collective-permute-start | bytes 2359304 | tf_op jit(solution)/shard_map/ppermute | solution.py:497
  751.9 164.9 %reduce-scatter.11.cloned.1.call-start = ((), (), s32[]{:S(2)}) async-start(), calls=%async_computation.39 | async-start | bytes 5242880 | tf_op jit(solution)/shard_map/reduce_scatter | solution.py:775
  756.3 43.8 %collective-permute-start.48 = (bf16[128,1408]{1,0:T(8,128)(2,1)}, bf16[128,1408]{1,0:T(8,128)(2,1)}, u32[]{:S(2)}, u32[]{:S(2)}) collective-permute-start(bf16[128,1408]{1,0:T(8,128)(2,1)} %get-tuple-element.336), channel_id=1, source_target_pairs={{0,1},{1,0},{2,3},{3,2},{4,5},{5,4},{6,7},{7,6},{8,9},{9,8},{10,11... | collective-permute-start | bytes 1081352 | tf_op jit(solution)/shard_map/ppermute | solution.py:501
  841.0 31.3 %collective-permute-start.58 = (bf16[256,1408]{1,0:T(8,128)(2,1)}, bf16[256,1408]{1,0:T(8,128)(2,1)}, u32[]{:S(2)}, u32[]{:S(2)}) collective-permute-start(bf16[256,1408]{1,0:T(8,128)(2,1)} %get-tuple-element.327), channel_id=1, source_target_pairs={{0,1},{1,0},{2,3},{3,2},{4,5},{5,4},{6,7},{7,6},{8,9},{9,8},{10,11... | collective-permute-start | bytes 2162696 | tf_op jit(solution)/shard_map/ppermute | solution.py:501
  843.0 31.7 %collective-permute-start.59 = (bf16[256,1408]{1,0:T(8,128)(2,1)}, bf16[256,1408]{1,0:T(8,128)(2,1)}, u32[]{:S(2)}, u32[]{:S(2)}) collective-permute-start(bf16[256,1408]{1,0:T(8,128)(2,1)} %get-tuple-element.326), channel_id=1, source_target_pairs={{0,2},{1,3},{2,0},{3,1},{4,6},{5,7},{6,4},{7,5},{8,10},{9,11},{10,... | collective-permute-start | bytes 2162696 | tf_op jit(solution)/shard_map/ppermute | solution.py:501
  844.5 38.2 %collective-permute-start.60 = (bf16[256,1408]{1,0:T(8,128)(2,1)}, bf16[256,1408]{1,0:T(8,128)(2,1)}, u32[]{:S(2)}, u32[]{:S(2)}) collective-permute-start(bf16[256,1408]{1,0:T(8,128)(2,1)} %get-tuple-element.325), channel_id=1, source_target_pairs={{0,3},{1,2},{2,1},{3,0},{4,7},{5,6},{6,5},{7,4},{8,11},{9,10},{10,... | collective-permute-start | bytes 2162696 | tf_op jit(solution)/shard_map/ppermute | solution.py:501
  856.8 44.5 %collective-permute-start.55 = (f32[2,7,512]{2,1,0:T(8,128)S(1)}, f32[2,7,512]{2,1,0:T(8,128)S(1)}, u32[]{:S(2)}, u32[]{:S(2)}) collective-permute-start(f32[2,7,512]{2,1,0:T(8,128)S(1)} %maximum_maximum_fusion), channel_id=1, source_target_pairs={{0,4},{4,0},{8,12},{12,8},{1,5},{5,1},{9,13},{13,9},{2,6},{6,2},{1... | collective-permute-start | bytes 86024 | tf_op jit(solution)/shard_map/ppermute | solution.py:501
  862.7 38.6 %collective-permute-start.56 = (f32[2,7,512]{2,1,0:T(8,128)S(1)}, f32[2,7,512]{2,1,0:T(8,128)S(1)}, u32[]{:S(2)}, u32[]{:S(2)}) collective-permute-start(f32[2,7,512]{2,1,0:T(8,128)S(1)} %maximum_maximum_fusion), channel_id=1, source_target_pairs={{0,8},{4,12},{8,0},{12,4},{1,9},{5,13},{9,1},{13,5},{2,10},{6,14},... | collective-permute-start | bytes 86024 | tf_op jit(solution)/shard_map/ppermute | solution.py:501
  (152 other events, 1770.5 us)
Sparse Core Ops, SparseCore 0:
  17.0 113.6 all-gather.10
  133.1 104.9 all-gather.6
  239.7 104.2 all-gather.12
  345.7 80.1 all-gather.8
  486.2 110.6 reduce-scatter.4
  599.0 93.5 reduce-scatter.6
  696.4 93.6 reduce-scatter.8
  831.3 82.1 reduce-scatter.10

commit v3 on v2

--- a/solution.py
+++ b/solution.py
@@ -471,8 +471,8 @@
     )
 
 
-def interleave(x):
-    _, n, f = x.shape
+def interleave(x, n):
+    f = x.shape[2]
     rows = 64 if n % 64 == 0 else n
 
     def body(_, x_ref, out_ref):
@@ -766,12 +766,17 @@
             d_parts = send_parts(d_wide[0], "col")
             g_home = trade(blocks, "col").reshape(dr, fc)
             g_home, sums, input_grads[0] = tie(g_home, sums, dx)
-            g_grads = unshare([g_home, place_all(g_late, me_c).reshape(dr, fc)])
+            g_grads = [g_home, place_all(g_late, me_c).reshape(dr, fc)]
             placed_back = to_output(input_grads)
             sums = jnp.concatenate([sums, jnp.stack(bias_sums)], axis=1)
             sums = total(add_all(send_all(sums, "row")), "section")
-            g_grads, *d_parts = tie(g_grads, *d_parts)
+            g_grads[0], *d_parts = tie(g_grads[0], *d_parts)
             d_grads[0] = add_all(d_parts).astype(BF)
+            if fc == fr:
+                g_grads = unshare([jnp.concatenate(pair) for pair in zip(g_grads, d_grads)])
+                d_grads = g_grads[:, dr:]
+            else:
+                g_grads, d_grads = unshare(g_grads), unshare(d_grads)
         pieces = [lax.psum_scatter(part, over, scatter_dimension=0, tiled=True) for part in wide_grads]
         qo_grads[layer] = jnp.concatenate(pieces, axis=1)
 
@@ -783,8 +788,8 @@
         jnp.stack(qo_grads[:3], axis=1)[None],
         sums[None, 4:],
         qo_grads[3][None],
-        interleave(g_grads)[None],
-        unshare(d_grads).astype(F32).reshape(dc, fr).T[None],
+        interleave(g_grads, dr)[None],
+        d_grads.astype(F32).reshape(dc, fr).T[None],
         sums[None, 0:2],
         sums[None, 2:4],
     )

time: 953 us -> 961 us (level)
  waiting for transfers between devices: 376 us -> 390 us
    all_to_all x22 -> x21, waiting for transfers between devices: 250 us -> 273 us  [trade(): return lax.all_to_all(stack, axis, split_axis=0, concat_axis=0)]
    ppermute x42, waiting for transfers between devices: 99.6 us -> 89.6 us  [hop(): lax.ppermute(value, axis, [(i, i ^ step) for i in range(lax.axis_size(axi...]
    all_to_all x22 -> x21, starting transfers between devices: 87 us -> 84 us  [trade(): return lax.all_to_all(stack, axis, split_axis=0, concat_axis=0)]
    unnamed x194 -> x188, local copies, waits for them, and re-layouts: 20.6 us -> 23.5 us
  transfers between devices with their start and end apart: 91 -> 90, of which waited for: 36 -> 35; matrix products, arithmetic and copies ran while one was open for 11% -> 10% of each run, Pallas kernels for 13% -> 12%
where the time goes in v3:
time: 961 us; the launch traced here: 949 us
  waiting for transfers between devices  390 us (41%)
  starting transfers between devices  185 us (19%)
  Pallas kernels  143 us (15%)
  local copies, waits for them, and re-layouts  101 us (11%)
  blocking collectives  81.7 us (9%)
  other arithmetic  31.3 us (3%)
  between operations  16.4 us (2%)
    all_to_all x21, waiting for transfers between devices, trade(): return lax.all_to_all(stack, axis, split_axis=0, concat_axis=0)  273 us
    pallas_call x17, Pallas kernels, call(): pl.pallas_call(body, grid_spec=pltpu.PrefetchScalarGridSpec(num_scalar_pr...  143 us
    ppermute x42, starting transfers between devices, hop(): lax.ppermute(value, axis, [(i, i ^ step) for i in range(lax.axis_size(axi...  96.2 us
    ppermute x42, waiting for transfers between devices, hop(): lax.ppermute(value, axis, [(i, i ^ step) for i in range(lax.axis_size(axi...  89.6 us
    all_to_all x21, starting transfers between devices, trade(): return lax.all_to_all(stack, axis, split_axis=0, concat_axis=0)  84 us
    all_to_all x8, blocking collectives, trade(): return lax.all_to_all(stack, axis, split_axis=0, concat_axis=0)  81.7 us
    dynamic_update_slice x36, local copies, waits for them, and re-layouts, place_all(): out = lax.dynamic_update_index_in_dim(out, piece, me ^ k, 0)  26.2 us
    unnamed x188, local copies, waits for them, and re-layouts  23.5 us
  transfers between devices with their start and end apart: 90, of which 35 were waited for; matrix products, arithmetic and copies ran while one was open for 10% of the time, Pallas kernels for 12%

profile of v3, /device:TPU:0, one launch (start us, length us, event | category | flops | bytes accessed | tf_op | source)
XLA Modules:
  0.0 948.7 jit_solution(9441154055265398242)
XLA Ops:
  81.9 22.2 %collective-permute-done.3 = bf16[128,1408]{1,0:T(8,128)(2,1)S(1)} collective-permute-done((bf16[128,1408]{1,0:T(8,128)(2,1)}, bf16[128,1408]{1,0:T(8,128)(2,1)S(1)}, u32[]{:S(2)}, u32[]{:S(2)}) %collective-permute-start.3) | collective-permute-done | bytes 360480 | tf_op jit(solution)/shard_map/ppermute | solution.py:501
  109.3 11.8 %collective-permute-done.5 = bf16[128,1408]{1,0:T(8,128)(2,1)S(1)} collective-permute-done((bf16[128,1408]{1,0:T(8,128)(2,1)S(1)}, bf16[128,1408]{1,0:T(8,128)(2,1)S(1)}, u32[]{:S(2)}, u32[]{:S(2)}) %collective-permute-start.5) | collective-permute-done | bytes 360480 | tf_op jit(solution)/shard_map/ppermute | solution.py:501
  133.3 9.3 all-to-all-done.5
  158.8 18.7 %collective-permute-start.10 = (bf16[128,1408]{1,0:T(8,128)(2,1)}, bf16[128,1408]{1,0:T(8,128)(2,1)S(1)}, u32[]{:S(2)}, u32[]{:S(2)}) collective-permute-start(bf16[128,1408]{1,0:T(8,128)(2,1)} %get-tuple-element.349), channel_id=1, source_target_pairs={{0,8},{4,12},{8,0},{12,4},{1,9},{5,13},{9,1},{13,5},{2,10},{6,14},... | collective-permute-start | bytes 1081352 | tf_op jit(solution)/shard_map/ppermute | solution.py:501
  188.7 13.4 %collective-permute-done.10 = bf16[128,1408]{1,0:T(8,128)(2,1)S(1)} collective-permute-done((bf16[128,1408]{1,0:T(8,128)(2,1)}, bf16[128,1408]{1,0:T(8,128)(2,1)S(1)}, u32[]{:S(2)}, u32[]{:S(2)}) %collective-permute-start.10) | collective-permute-done | bytes 360480 | tf_op jit(solution)/shard_map/ppermute | solution.py:501
  202.1 12.0 %all_to_all.146 = bf16[4,64,512]{2,1,0:T(8,128)(2,1)S(1)} all-to-all(bf16[4,64,512]{2,1,0:T(8,128)(2,1)} %bitcast.407), channel_id=1, replica_groups=mesh['section'=2,'row'=4,'col'=4] {'col'}, dimensions={0} | all-to-all | bytes 524288 | tf_op jit(solution)/shard_map/all_to_all | solution.py:19
  226.6 21.7 %all-to-all-done.8 = bf16[4,64,2048]{2,1,0:T(8,128)(2,1)S(1)} async-done(((bf16[4,64,2048]{2,1,0:T(8,128)(2,1)}), bf16[4,64,2048]{2,1,0:T(8,128)(2,1)S(1)}, u32[]{:S(2)}, u32[]{:S(2)}) %all-to-all-start.8) | async-done | bytes 1048608 | tf_op jit(solution)/shard_map/all_to_all | solution.py:19
  249.3 11.4 %shard_map.180 = (f32[256,1408]{1,0:T(8,128)}, f32[256,1408]{1,0:T(8,128)}, bf16[256,1408]{1,0:T(8,128)(2,1)}, bf16[256,2048]{1,0:T(8,128)(2,1)}) custom-call(s32[1,2]{1,0:T(1,128)} %iota.25.t, bf16[256,2048]{1,0:T(8,128)(2,1)} %bitcast.382, bf16[2,4,3,256,1408]{4,3,2,1,0:T(8,128)(2,1)} %bitcast.351), custom_call_target="tpu_custom_call" | custom-call | flops 4429185024 | bytes 17301504 | tf_op jit(solution)/shard_map/pallas_call | solution.py:63
  268.0 50.8 %all-to-all-done.10 = bf16[4,64,2048]{2,1,0:T(8,128)(2,1)S(1)} async-done(((bf16[4,64,2048]{2,1,0:T(8,128)(2,1)}), bf16[4,64,2048]{2,1,0:T(8,128)(2,1)S(1)}, u32[]{:S(2)}, u32[]{:S(2)}) %all-to-all-start.10) | async-done | bytes 1048608 | tf_op jit(solution)/shard_map/all_to_all | solution.py:19
  327.7 16.3 %all-gather.13.cloned.1.call-done = bf16[1,2048,2048]{2,1,0:T(8,128)(2,1)} async-done(((bf16[1,256,2048]{2,1,0:T(8,128)(2,1)}), bf16[1,2048,2048]{2,1,0:T(8,128)(2,1)}) %all-gather.13.cloned.1.call-update) | async-done | bytes 8388624 | tf_op jit(solution)/shard_map/all_gather | solution.py:583
  364.7 17.2 %all-to-all-done.12.o_ref = bf16[4,256,512]{2,1,0:T(8,128)(2,1)} async-done(((bf16[4,256,512]{2,1,0:T(8,128)(2,1)}), bf16[4,256,512]{2,1,0:T(8,128)(2,1)}, u32[]{:S(2)}, u32[]{:S(2)}) %all-to-all-start.12) | async-done | bytes 1048608 | tf_op jit(solution)/shard_map/all_to_all | solution.py:19
  391.2 7.6 all-to-all-done.13
  413.3 17.6 %all-to-all-done.14 = bf16[4,64,2048]{2,1,0:T(8,128)(2,1)} async-done(((bf16[4,64,2048]{2,1,0:T(8,128)(2,1)}), bf16[4,64,2048]{2,1,0:T(8,128)(2,1)}, u32[]{:S(2)}, u32[]{:S(2)}) %all-to-all-start.14) | async-done | bytes 1048608 | tf_op jit(solution)/shard_map/all_to_all | solution.py:19
  430.9 11.5 %shard_map.183 = (f32[256,1408]{1,0:T(8,128)}, f32[256,1408]{1,0:T(8,128)}, bf16[256,1408]{1,0:T(8,128)(2,1)}, bf16[256,2048]{1,0:T(8,128)(2,1)}) custom-call(s32[1,2]{1,0:T(1,128)} %iota_xor_fusion.t, bf16[256,2048]{1,0:T(8,128)(2,1)} %bitcast.79.b_ref, bf16[2,4,2,256,1408]{4,3,2,1,0:T(8,128)(2,1)} %bitcast.353, bf16[4,256,1408]{2,1,0:T(8,128)(2,1)} %copy-done, ...), custom_call_target="tpu_custom_call" | custom-call | flops 4429185024 | bytes 17301504 | tf_op jit(solution)/shard_map/pallas_call | solution.py:63
  442.4 13.2 %shard_map.184 = (bf16[2,256,1408]{2,1,0:T(8,128)(2,1)}, bf16[256,2048]{1,0:T(8,128)(2,1)}) custom-call(s32[1,2]{1,0:T(1,128)} %iota_xor_fusion.t, bf16[256,2048]{1,0:T(8,128)(2,1)} %bitcast.76.dy_ref, f32[256,1408]{1,0:T(8,128)} %get-tuple-element.186.gate_ref, f32[256,1408]{1,0:T(8,128)} %get-tuple-element.187.up_ref, ...), custom_call_target="tpu_custom_call" | custom-call | flops 4429185024 | bytes 17301504 | tf_op jit(solution)/shard_map/pallas_call | solution.py:63
  466.6 10.0 %shard_map.185 = bf16[4,768,1408]{2,1,0:T(8,128)(2,1)} custom-call(s32[1,1]{1,0:T(1,128)} %bitcast.91._, bf16[256,2048]{1,0:T(8,128)(2,1)} %bitcast.79.b_ref, bf16[2,256,1408]{2,1,0:T(8,128)(2,1)} %get-tuple-element.193.d_ref, bf16[256,2048]{1,0:T(8,128)(2,1)} %bitcast.76.dy_ref, bf16[256,1408]{1,0:T(8,128)(2,1)} %get-tuple-element.195.m_ref, ...), custom_call_target="tpu_custom_call" | custom-call | flops 4429185024 | bytes 8650752 | tf_op jit(solution)/shard_map/pallas_call | solution.py:63
  476.6 9.2 all-to-all-done.15
  488.1 11.8 %all_to_all.147 = bf16[4,64,512]{2,1,0:T(8,128)(2,1)} all-to-all(bf16[4,64,512]{2,1,0:T(8,128)(2,1)S(1)} %copy.123), channel_id=1, replica_groups=mesh['section'=2,'row'=4,'col'=4] {'col'}, dimensions={0} | all-to-all | bytes 524288 | tf_op jit(solution)/shard_map/all_to_all | solution.py:19
  514.7 18.5 %all-to-all-done.17 = bf16[4,256,512]{2,1,0:T(8,128)(2,1)S(1)} async-done(((bf16[4,256,512]{2,1,0:T(8,128)(2,1)}), bf16[4,256,512]{2,1,0:T(8,128)(2,1)S(1)}, u32[]{:S(2)}, u32[]{:S(2)}) %all-to-all-start.17) | async-done | bytes 1048608 | tf_op jit(solution)/shard_map/all_to_all | solution.py:19
  534.7 9.2 shard_map.187
  548.8 15.8 %all-to-all-done.18 = bf16[4,64,2048]{2,1,0:T(8,128)(2,1)S(1)} async-done(((bf16[4,64,2048]{2,1,0:T(8,128)(2,1)}), bf16[4,64,2048]{2,1,0:T(8,128)(2,1)S(1)}, u32[]{:S(2)}, u32[]{:S(2)}) %all-to-all-start.18) | async-done | bytes 1048608 | tf_op jit(solution)/shard_map/all_to_all | solution.py:19
  574.3 28.7 %all_to_all.148 = bf16[4,64,2048]{2,1,0:T(8,128)(2,1)} all-to-all(bf16[4,64,2048]{2,1,0:T(8,128)(2,1)S(1)} %broadcast_in_dim.236), channel_id=1, replica_groups=mesh['section'=2,'row'=4,'col'=4] {'row'}, dimensions={0} | all-to-all | bytes 2097152 | tf_op jit(solution)/shard_map/all_to_all | solution.py:19
  603.5 14.0 %shard_map.189 = (bf16[2,256,1408]{2,1,0:T(8,128)(2,1)}, bf16[256,2048]{1,0:T(8,128)(2,1)}) custom-call(s32[1,2]{1,0:T(1,128)} %iota.28.t, bf16[256,2048]{1,0:T(8,128)(2,1)} %bitcast.379, f32[256,1408]{1,0:T(8,128)} %get-tuple-element.205.gate_ref, f32[256,1408]{1,0:T(8,128)} %get-tuple-element.206.up_ref, bf16[2,4,3,256,1408]{4,3,2,1,0:T(8,128)(2,1)} %bitcast.352), custom_call_target="tpu_custom_call" | custom-call | flops 4429185024 | bytes 17301504 | tf_op jit(solution)/shard_map/pallas_call | solution.py:63
  630.7 9.6 %shard_map.190 = (bf16[4,512,1408]{2,1,0:T(8,128)(2,1)}, bf16[4,256,1408]{2,1,0:T(8,128)(2,1)}) custom-call(s32[1,1]{1,0:T(1,128)} %bitcast.91._, bf16[256,2048]{1,0:T(8,128)(2,1)} %bitcast.384, bf16[2,256,1408]{2,1,0:T(8,128)(2,1)} %get-tuple-element.214.d_ref, bf16[256,2048]{1,0:T(8,128)(2,1)} %bitcast.380, bf16[256,1408]{1,0:T(8,128)(2,1)} %get-tuple-element.216.m_ref, ...), custom_call_target="tpu_custom_call" | custom-call | flops 4429185024 | bytes 8650752 | tf_op jit(solution)/shard_map/pallas_call | solution.py:63
  640.3 36.4 %all-to-all-done.20 = bf16[4,64,2048]{2,1,0:T(8,128)(2,1)S(1)} async-done(((bf16[4,64,2048]{2,1,0:T(8,128)(2,1)}), bf16[4,64,2048]{2,1,0:T(8,128)(2,1)S(1)}, u32[]{:S(2)}, u32[]{:S(2)}) %all-to-all-start.20) | async-done | bytes 1048608 | tf_op jit(solution)/shard_map/all_to_all | solution.py:19
  714.1 9.1 all-to-all-done.22
  724.1 14.0 %collective-permute-done.39 = bf16[128,1408]{1,0:T(8,128)(2,1)} collective-permute-done((bf16[128,1408]{1,0:T(8,128)(2,1)}, bf16[128,1408]{1,0:T(8,128)(2,1)}, u32[]{:S(2)}, u32[]{:S(2)}) %collective-permute-start.39) | collective-permute-done | bytes 360480 | tf_op jit(solution)/shard_map/ppermute | solution.py:501
  738.1 9.2 shard_map.192
  758.8 17.9 %all-to-all-done.23 = bf16[4,64,2048]{2,1,0:T(8,128)(2,1)} async-done(((bf16[4,64,2048]{2,1,0:T(8,128)(2,1)}), bf16[4,64,2048]{2,1,0:T(8,128)(2,1)}, u32[]{:S(2)}, u32[]{:S(2)}) %all-to-all-start.23) | async-done | bytes 1048608 | tf_op jit(solution)/shard_map/all_to_all | solution.py:19
  812.9 14.1 %collective-permute-done.46 = bf16[128,1408]{1,0:T(8,128)(2,1)S(1)} collective-permute-done((bf16[128,1408]{1,0:T(8,128)(2,1)S(1)}, bf16[128,1408]{1,0:T(8,128)(2,1)S(1)}, u32[]{:S(2)}, u32[]{:S(2)}) %collective-permute-start.46) | collective-permute-done | bytes 360480 | tf_op jit(solution)/shard_map/ppermute | solution.py:501
  846.7 33.0 %all-to-all-done.25 = bf16[4,128,1408]{2,1,0:T(8,128)(2,1)} async-done(((bf16[4,128,1408]{2,1,0:T(8,128)(2,1)}), bf16[4,128,1408]{2,1,0:T(8,128)(2,1)}, u32[]{:S(2)}, u32[]{:S(2)}) %all-to-all-start.25) | async-done | bytes 1441824 | tf_op jit(solution)/shard_map/all_to_all | solution.py:19
  879.7 8.4 collective-permute-start.55
  (563 shorter events, 409.1 us)
Async XLA Ops:
  7.2 135.3 %all-gather.11.cloned.1.call-start = ((), (), s32[]{:S(2)}) async-start(), calls=%async_computation.39 | async-start | bytes 9437184 | tf_op jit(solution)/shard_map/all_gather | solution.py:583
  39.3 38.8 %collective-permute-start.6 = (bf16[128,1408]{1,0:T(8,128)(2,1)}, bf16[128,1408]{1,0:T(8,128)(2,1)}, u32[]{:S(2)}, u32[]{:S(2)}) collective-permute-start(bf16[128,1408]{1,0:T(8,128)(2,1)} %get-tuple-element.354), channel_id=1, source_target_pairs={{0,1},{1,0},{2,3},{3,2},{4,5},{5,4},{6,7},{7,6},{8,9},{9,8},{10,11... | collective-permute-start | bytes 1081352 | tf_op jit(solution)/shard_map/ppermute | solution.py:501
  41.3 40.6 %collective-permute-start.7 = (bf16[128,1408]{1,0:T(8,128)(2,1)}, bf16[128,1408]{1,0:T(8,128)(2,1)}, u32[]{:S(2)}, u32[]{:S(2)}) collective-permute-start(bf16[128,1408]{1,0:T(8,128)(2,1)} %get-tuple-element.353), channel_id=1, source_target_pairs={{0,2},{1,3},{2,0},{3,1},{4,6},{5,7},{6,4},{7,5},{8,10},{9,11},{10,... | collective-permute-start | bytes 1081352 | tf_op jit(solution)/shard_map/ppermute | solution.py:501
  68.3 180.0 %all-gather.7.cloned.1.call-start = ((), (), s32[]{:S(2)}) async-start(), calls=%async_computation.33 | async-start | bytes 19464192 | tf_op jit(solution)/shard_map/all_gather | solution.py:596
  69.4 34.7 %collective-permute-start.3 = (bf16[128,1408]{1,0:T(8,128)(2,1)}, bf16[128,1408]{1,0:T(8,128)(2,1)S(1)}, u32[]{:S(2)}, u32[]{:S(2)}) collective-permute-start(bf16[128,1408]{1,0:T(8,128)(2,1)} %get-tuple-element.358), channel_id=1, source_target_pairs={{0,4},{4,0},{8,12},{12,8},{1,5},{5,1},{9,13},{13,9},{2,6},{6,2},{1... | collective-permute-start | bytes 1081352 | tf_op jit(solution)/shard_map/ppermute | solution.py:501
  71.0 38.3 %collective-permute-start.4 = (bf16[128,1408]{1,0:T(8,128)(2,1)}, bf16[128,1408]{1,0:T(8,128)(2,1)}, u32[]{:S(2)}, u32[]{:S(2)}) collective-permute-start(bf16[128,1408]{1,0:T(8,128)(2,1)} %get-tuple-element.357), channel_id=1, source_target_pairs={{0,8},{4,12},{8,0},{12,4},{1,9},{5,13},{9,1},{13,5},{2,10},{6,14},... | collective-permute-start | bytes 1081352 | tf_op jit(solution)/shard_map/ppermute | solution.py:501
  78.1 43.0 %collective-permute-start.5 = (bf16[128,1408]{1,0:T(8,128)(2,1)S(1)}, bf16[128,1408]{1,0:T(8,128)(2,1)S(1)}, u32[]{:S(2)}, u32[]{:S(2)}) collective-permute-start(bf16[128,1408]{1,0:T(8,128)(2,1)S(1)} %get-tuple-element.356), channel_id=1, source_target_pairs={{0,12},{4,8},{8,4},{12,0},{1,13},{5,9},{9,5},{13,1},{2,14},{6,10},... | collective-permute-start | bytes 1081352 | tf_op jit(solution)/shard_map/ppermute | solution.py:501
  156.6 187.4 %all-gather.13.cloned.1.call-start = ((), (), s32[]{:S(2)}) async-start(), calls=%async_computation.40 | async-start | bytes 9437184 | tf_op jit(solution)/shard_map/all_gather | solution.py:583
  158.8 43.2 %collective-permute-start.10 = (bf16[128,1408]{1,0:T(8,128)(2,1)}, bf16[128,1408]{1,0:T(8,128)(2,1)S(1)}, u32[]{:S(2)}, u32[]{:S(2)}) collective-permute-start(bf16[128,1408]{1,0:T(8,128)(2,1)} %get-tuple-element.349), channel_id=1, source_target_pairs={{0,8},{4,12},{8,0},{12,4},{1,9},{5,13},{9,1},{13,5},{2,10},{6,14},... | collective-permute-start | bytes 1081352 | tf_op jit(solution)/shard_map/ppermute | solution.py:501
  225.4 205.6 %all-gather.9.cloned.1.call-start = ((), (), s32[]{:S(2)}) async-start(), calls=%async_computation.34 | async-start | bytes 12976128 | tf_op jit(solution)/shard_map/all_gather | solution.py:596
  260.7 58.1 %all-to-all-start.10 = ((bf16[4,64,2048]{2,1,0:T(8,128)(2,1)}), bf16[4,64,2048]{2,1,0:T(8,128)(2,1)S(1)}, u32[]{:S(2)}, u32[]{:S(2)}) async-start(bf16[4,64,2048]{2,1,0:T(8,128)(2,1)} %bitcast.411), calls=%async_computation.10 | async-start | bytes 2097152 | tf_op jit(solution)/shard_map/all_to_all | solution.py:19
  264.4 54.6 %collective-permute-start.12 = (bf16[256,1408]{1,0:T(8,128)(2,1)S(1)}, bf16[256,1408]{1,0:T(8,128)(2,1)}, u32[]{:S(2)}, u32[]{:S(2)}) collective-permute-start(bf16[256,1408]{1,0:T(8,128)(2,1)S(1)} %copy-done.17), channel_id=1, source_target_pairs={{0,1},{1,0},{2,3},{3,2},{4,5},{5,4},{6,7},{7,6},{8,9},{9,8},{10,11... | collective-permute-start | bytes 2162696 | tf_op jit(solution)/shard_map/ppermute | solution.py:501
  265.7 53.3 %collective-permute-start.13 = (bf16[256,1408]{1,0:T(8,128)(2,1)S(1)}, bf16[256,1408]{1,0:T(8,128)(2,1)}, u32[]{:S(2)}, u32[]{:S(2)}) collective-permute-start(bf16[256,1408]{1,0:T(8,128)(2,1)S(1)} %copy-done.17), channel_id=1, source_target_pairs={{0,2},{1,3},{2,0},{3,1},{4,6},{5,7},{6,4},{7,5},{8,10},{9,11},{10,... | collective-permute-start | bytes 2162696 | tf_op jit(solution)/shard_map/ppermute | solution.py:501
  266.5 52.5 %collective-permute-start.14 = (bf16[256,1408]{1,0:T(8,128)(2,1)S(1)}, bf16[256,1408]{1,0:T(8,128)(2,1)S(1)}, u32[]{:S(2)}, u32[]{:S(2)}) collective-permute-start(bf16[256,1408]{1,0:T(8,128)(2,1)S(1)} %copy-done.17), channel_id=1, source_target_pairs={{0,3},{1,2},{2,1},{3,0},{4,7},{5,6},{6,5},{7,4},{8,11},{9,10},{10,... | collective-permute-start | bytes 2162696 | tf_op jit(solution)/shard_map/ppermute | solution.py:501
  459.2 158.3 %reduce-scatter.5.cloned.1.call-start = ((), (), s32[]{:S(2)}) async-start(), calls=%async_computation.35 | async-start | bytes 10813440 | tf_op jit(solution)/shard_map/reduce_scatter | solution.py:724
  514.1 50.6 %collective-permute-start.26 = (bf16[256,2048]{1,0:T(8,128)(2,1)}, bf16[256,2048]{1,0:T(8,128)(2,1)}, u32[]{:S(2)}, u32[]{:S(2)}) collective-permute-start(bf16[256,2048]{1,0:T(8,128)(2,1)} %bitcast.68.a_ref), channel_id=1, source_target_pairs={{0,16},{16,0},{1,17},{17,1},{2,18},{18,2},{3,19},{19,3},{4,20},{20... | collective-permute-start | bytes 3145736 | tf_op jit(solution)/shard_map/ppermute | solution.py:497
  514.1 50.6 %collective-permute-start.27 = (bf16[4,256,512]{2,1,0:T(8,128)(2,1)}, bf16[4,256,512]{2,1,0:T(8,128)(2,1)}, u32[]{:S(2)}, u32[]{:S(2)}) collective-permute-start(bf16[4,256,512]{2,1,0:T(8,128)(2,1)} %all-to-all-done.12.o_ref), channel_id=1, source_target_pairs={{0,16},{16,0},{1,17},{17,1},{2,18},{18,2},{3,19},{19,3},{4,20},{20... | collective-permute-start | bytes 3145736 | tf_op jit(solution)/shard_map/ppermute | solution.py:497
  547.7 176.4 %reduce-scatter.7.cloned.1.call-start = ((), (), s32[]{:S(2)}) async-start(), calls=%async_computation.36 | async-start | bytes 5242880 | tf_op jit(solution)/shard_map/reduce_scatter | solution.py:780
  620.2 56.5 %all-to-all-start.20 = ((bf16[4,64,2048]{2,1,0:T(8,128)(2,1)}), bf16[4,64,2048]{2,1,0:T(8,128)(2,1)S(1)}, u32[]{:S(2)}, u32[]{:S(2)}) async-start(bf16[4,64,2048]{2,1,0:T(8,128)(2,1)} %bitcast.408), calls=%async_computation.21 | async-start | bytes 2097152 | tf_op jit(solution)/shard_map/all_to_all | solution.py:19
  623.8 166.9 %reduce-scatter.9.cloned.1.call-start = ((), (), s32[]{:S(2)}) async-start(), calls=%async_computation.37 | async-start | bytes 7208960 | tf_op jit(solution)/shard_map/reduce_scatter | solution.py:724
  691.6 86.6 %collective-permute-start.41 = (bf16[256,2048]{1,0:T(8,128)(2,1)S(1)}, bf16[256,2048]{1,0:T(8,128)(2,1)}, u32[]{:S(2)}, u32[]{:S(2)}) collective-permute-start(bf16[256,2048]{1,0:T(8,128)(2,1)S(1)} %bitcast.363), channel_id=1, source_target_pairs={{0,16},{16,0},{1,17},{17,1},{2,18},{18,2},{3,19},{19,3},{4,20},{20... | collective-permute-start | bytes 3145736 | tf_op jit(solution)/shard_map/ppermute | solution.py:497
  691.6 88.0 %collective-permute-start.42 = (bf16[4,256,512]{2,1,0:T(8,128)(2,1)S(1)}, bf16[4,256,512]{2,1,0:T(8,128)(2,1)}, u32[]{:S(2)}, u32[]{:S(2)}) collective-permute-start(bf16[4,256,512]{2,1,0:T(8,128)(2,1)S(1)} %copy-done.5), channel_id=1, source_target_pairs={{0,16},{16,0},{1,17},{17,1},{2,18},{18,2},{3,19},{19,3},{4,20},{20... | collective-permute-start | bytes 3145736 | tf_op jit(solution)/shard_map/ppermute | solution.py:497
  706.9 31.1 %collective-permute-start.39 = (bf16[128,1408]{1,0:T(8,128)(2,1)}, bf16[128,1408]{1,0:T(8,128)(2,1)}, u32[]{:S(2)}, u32[]{:S(2)}) collective-permute-start(bf16[128,1408]{1,0:T(8,128)(2,1)} %get-tuple-element.343), channel_id=1, source_target_pairs={{0,8},{4,12},{8,0},{12,4},{1,9},{5,13},{9,1},{13,5},{2,10},{6,14},... | collective-permute-start | bytes 1081352 | tf_op jit(solution)/shard_map/ppermute | solution.py:501
  724.1 57.0 %collective-permute-start.44 = (bf16[256,512]{1,0:T(8,128)(2,1)}, bf16[256,512]{1,0:T(8,128)(2,1)S(1)}, u32[]{:S(2)}, u32[]{:S(2)}) collective-permute-start(bf16[256,512]{1,0:T(8,128)(2,1)} %bitcast.392), channel_id=1, source_target_pairs={{0,16},{16,0},{1,17},{17,1},{2,18},{18,2},{3,19},{19,3},{4,20},{20... | collective-permute-start | bytes 786440 | tf_op jit(solution)/shard_map/ppermute | solution.py:497
  747.3 33.8 %collective-permute-start.43 = (bf16[256,1536]{1,0:T(8,128)(2,1)}, bf16[256,1536]{1,0:T(8,128)(2,1)}, u32[]{:S(2)}, u32[]{:S(2)}) collective-permute-start(bf16[256,1536]{1,0:T(8,128)(2,1)} %get-tuple-element.231.dp_ref), channel_id=1, source_target_pairs={{0,16},{16,0},{1,17},{17,1},{2,18},{18,2},{3,19},{19,3},{4,20},{20... | collective-permute-start | bytes 2359304 | tf_op jit(solution)/shard_map/ppermute | solution.py:497
  752.1 178.3 %reduce-scatter.11.cloned.1.call-start = ((), (), s32[]{:S(2)}) async-start(), calls=%async_computation.38 | async-start | bytes 5242880 | tf_op jit(solution)/shard_map/reduce_scatter | solution.py:780
  756.6 43.7 %collective-permute-start.48 = (bf16[128,1408]{1,0:T(8,128)(2,1)}, bf16[128,1408]{1,0:T(8,128)(2,1)}, u32[]{:S(2)}, u32[]{:S(2)}) collective-permute-start(bf16[128,1408]{1,0:T(8,128)(2,1)} %get-tuple-element.336), channel_id=1, source_target_pairs={{0,1},{1,0},{2,3},{3,2},{4,5},{5,4},{6,7},{7,6},{8,9},{9,8},{10,11... | collective-permute-start | bytes 1081352 | tf_op jit(solution)/shard_map/ppermute | solution.py:501
  835.2 53.9 %collective-permute-start.58 = (bf16[256,1408]{1,0:T(8,128)(2,1)}, bf16[256,1408]{1,0:T(8,128)(2,1)}, u32[]{:S(2)}, u32[]{:S(2)}) collective-permute-start(bf16[256,1408]{1,0:T(8,128)(2,1)} %get-tuple-element.327), channel_id=1, source_target_pairs={{0,1},{1,0},{2,3},{3,2},{4,5},{5,4},{6,7},{7,6},{8,9},{9,8},{10,11... | collective-permute-start | bytes 2162696 | tf_op jit(solution)/shard_map/ppermute | solution.py:501
  835.8 54.7 %collective-permute-start.59 = (bf16[256,1408]{1,0:T(8,128)(2,1)}, bf16[256,1408]{1,0:T(8,128)(2,1)}, u32[]{:S(2)}, u32[]{:S(2)}) collective-permute-start(bf16[256,1408]{1,0:T(8,128)(2,1)} %get-tuple-element.326), channel_id=1, source_target_pairs={{0,2},{1,3},{2,0},{3,1},{4,6},{5,7},{6,4},{7,5},{8,10},{9,11},{10,... | collective-permute-start | bytes 2162696 | tf_op jit(solution)/shard_map/ppermute | solution.py:501
  837.2 53.3 %collective-permute-start.60 = (bf16[256,1408]{1,0:T(8,128)(2,1)}, bf16[256,1408]{1,0:T(8,128)(2,1)}, u32[]{:S(2)}, u32[]{:S(2)}) collective-permute-start(bf16[256,1408]{1,0:T(8,128)(2,1)} %get-tuple-element.325), channel_id=1, source_target_pairs={{0,3},{1,2},{2,1},{3,0},{4,7},{5,6},{6,5},{7,4},{8,11},{9,10},{10,... | collective-permute-start | bytes 2162696 | tf_op jit(solution)/shard_map/ppermute | solution.py:501
  838.7 41.0 %all-to-all-start.25 = ((bf16[4,128,1408]{2,1,0:T(8,128)(2,1)}), bf16[4,128,1408]{2,1,0:T(8,128)(2,1)}, u32[]{:S(2)}, u32[]{:S(2)}) async-start(bf16[4,128,1408]{2,1,0:T(8,128)(2,1)} %bitcast_dynamic-update-slice_fusion.8), calls=%async_computation.28 | async-start | bytes 2883584 | tf_op jit(solution)/shard_map/all_to_all | solution.py:19
  879.7 34.3 %collective-permute-start.55 = (f32[2,7,512]{2,1,0:T(8,128)S(1)}, f32[2,7,512]{2,1,0:T(8,128)S(1)}, u32[]{:S(2)}, u32[]{:S(2)}) collective-permute-start(f32[2,7,512]{2,1,0:T(8,128)S(1)} %maximum_maximum_fusion), channel_id=1, source_target_pairs={{0,4},{4,0},{8,12},{12,8},{1,5},{5,1},{9,13},{13,9},{2,6},{6,2},{1... | collective-permute-start | bytes 86024 | tf_op jit(solution)/shard_map/ppermute | solution.py:501
  (149 other events, 1724.1 us)
Sparse Core Ops, SparseCore 0:
  17.0 113.6 all-gather.10
  133.1 104.9 all-gather.6
  239.7 104.2 all-gather.12
  345.7 80.1 all-gather.8
  486.2 110.6 reduce-scatter.4
  599.0 93.5 reduce-scatter.6
  696.5 93.7 reduce-scatter.8
  831.4 82.1 reduce-scatter.10
